TPU v7x, 32 devices: a whole 2x2x4 slice. The times are simulated.
32 devices in a mesh: groups: 2 (over x), tile: 16 (over z, y, core).
Axes of the slice: x: 2, y: 2, z: 4, core: 2. Of those that a mesh axis runs over, the one named last changes fastest.
Arguments:
- ref_feat: bfloat16 [64, 256, 256], P('groups', 'tile'), parts along dimension 0, may hold values from -6 to 6
- src_feat: bfloat16 [8, 32, 256, 256], P('groups', None, 'tile'), parts along dimension 0, may hold values from -6 to 6
- row_tap: int32 [8, 32, 256], P('groups', None, 'tile'), parts along dimension 0, may hold values from 0 to 254, as said below
- row_frac: bfloat16 [8, 32, 256], P('groups', None, 'tile'), parts along dimension 0, may hold values from 0 to 1
- col_tap: int32 [8, 32, 256], P('groups'), parts along dimension 0, may hold values from 0 to 254
- col_frac: bfloat16 [8, 32, 256], P('groups'), parts along dimension 0, may hold values from 0 to 1
- view_count: int32 [32], P(('groups', 'tile')), parts along dimension 0, may hold values from 1 to 4
- conv_weight: bfloat16 [3, 3, 3, 8, 32], replicated, may hold values from -0.21875 to 0.21875
- conv_bias: float32 [8], replicated, may hold values from -1 to 1
Outputs:
- cost_volume: bfloat16 [64, 8, 256, 256], P('groups', None, 'tile'), parts along dimension 0
There are 2 independent parts, one for each index of `groups`. A program takes and returns all parts, laid end to end along the dimension named above; an argument that names none is the same for every part. Nothing has to cross between parts.
Inputs may be any that keep to these rules, and one draw needn't show every extreme that they name: For reference rows of strip t (rows t * 16 to (t + 1) * 16 - 1), row_tap and row_tap + 1 lie in rows max(0, (t - 2) * 16) to min(256, (t + 3) * 16) - 1.
All inputs are finite; a program needn't handle non-finite values.
Results may differ from a plain program's by a relative error of at most 0.0051.
Values may be sent and summed in bfloat16 or wider, within the bound.
No kernel may reach another device: no remote copies, remote signals or barrier semaphores. Data moves between devices by JAX's collectives and lax.ppermute only.
A program may use at most 192 MiB of HBM per device.

v0:
```python
import jax
import jax.numpy as jnp
from jax import lax
from jax.sharding import PartitionSpec as P

REACH = 2


def shifted(x, axis, by):
    length = lax.axis_size(axis)
    pairs = [(i, i + by) for i in range(length) if 0 <= i + by < length]
    return lax.ppermute(x, axis, pairs)


def extended(block, sides, width):
    for axis, dim in sides:
        count = lax.axis_size(axis)
        forward = [(i, i + 1) for i in range(count - 1)]
        backward = [(target, source) for source, target in forward]
        low = lax.ppermute(
            lax.slice_in_dim(block, block.shape[dim] - width, None, axis=dim), axis, forward
        )
        high = lax.ppermute(lax.slice_in_dim(block, 0, width, axis=dim), axis, backward)
        block = jnp.concatenate([low, block, high], axis=dim)
    return block


def stacked_columns_all(stack):
    width = stack.shape[3]
    padded = jnp.pad(stack, ((0, 0), (0, 0), (0, 0), (1, 1)))
    return jnp.concatenate(
        [padded[:, :, :, 0:width], padded[:, :, :, 1 : width + 1], padded[:, :, :, 2 : width + 2]],
        axis=1,
    )


def stack_term(padded, weight_mats, offset, planes):
    total = jnp.einsum(
        "oc,pcrw->porw",
        weight_mats[0, offset],
        padded[0:planes],
        preferred_element_type=jnp.float32,
    )
    for depth_tap in range(1, 3):
        total = total + jnp.einsum(
            "oc,pcrw->porw",
            weight_mats[depth_tap, offset],
            padded[depth_tap : depth_tap + planes],
            preferred_element_type=jnp.float32,
        )
    return total


def on_device(
    ref_feat, src_feat, row_tap, row_frac, col_tap, col_frac, view_count, conv_weight, conv_bias
):
    channels = ref_feat.shape[0]
    strip_rows = ref_feat.shape[1]
    columns = ref_feat.shape[2]
    sources = src_feat.shape[0]
    planes = row_tap.shape[1]
    out_channels = conv_weight.shape[3]
    before_list = []
    after_list = []
    for distance in range(1, REACH + 1):
        before_list.append(shifted(src_feat, "tile", distance))
        after_list.append(shifted(src_feat, "tile", -distance))
    band_rows = jnp.concatenate(before_list[::-1] + [src_feat] + after_list, axis=2)
    band_length = band_rows.shape[2]
    band_start = (lax.axis_index("tile") - REACH) * strip_rows
    local_taps = row_tap - band_start
    band_index = jnp.arange(band_length, dtype=jnp.int32)
    col_index = jnp.arange(columns, dtype=jnp.int32)
    row_keep = (1.0 - row_frac.astype(jnp.float32)).astype(jnp.bfloat16)
    col_keep = (1.0 - col_frac.astype(jnp.float32)).astype(jnp.bfloat16)
    zero_weight = jnp.zeros((), jnp.bfloat16)
    valid = (jnp.arange(sources) < view_count[0]).astype(jnp.float32)
    divisor = 1.0 + view_count[0].astype(jnp.float32)
    base = ref_feat.astype(jnp.float32)
    weight_mats = jnp.transpose(conv_weight, (0, 1, 3, 2, 4)).reshape(
        3, 3, out_channels, 3 * channels
    )

    def plane_variance(depth):
        taps = lax.dynamic_index_in_dim(local_taps, depth, 1, keepdims=False)
        keep_rows = lax.dynamic_index_in_dim(row_keep, depth, 1, keepdims=False)
        frac_rows = lax.dynamic_index_in_dim(row_frac, depth, 1, keepdims=False)
        row_matrix = jnp.where(
            band_index[None, None, :] == taps[:, :, None],
            keep_rows[:, :, None],
            jnp.where(
                band_index[None, None, :] == taps[:, :, None] + 1,
                frac_rows[:, :, None],
                zero_weight,
            ),
        )
        rowmix = jnp.einsum(
            "vrb,vcbw->vcrw", row_matrix, band_rows, preferred_element_type=jnp.float32
        ).astype(jnp.bfloat16)
        col_taps = lax.dynamic_index_in_dim(col_tap, depth, 1, keepdims=False)
        keep_cols = lax.dynamic_index_in_dim(col_keep, depth, 1, keepdims=False)
        frac_cols = lax.dynamic_index_in_dim(col_frac, depth, 1, keepdims=False)
        col_matrix = jnp.where(
            col_index[None, :, None] == col_taps[:, None, :],
            keep_cols[:, None, :],
            jnp.where(
                col_index[None, :, None] == col_taps[:, None, :] + 1,
                frac_cols[:, None, :],
                zero_weight,
            ),
        )
        warped = jnp.einsum(
            "vcrw,vwk->vcrk", rowmix, col_matrix, preferred_element_type=jnp.float32
        )
        masked = warped * valid[:, None, None, None]
        total = base + jnp.sum(masked, axis=0)
        squares = base * base + jnp.sum(masked * warped, axis=0)
        mean_value = total / divisor
        return (squares / divisor - mean_value * mean_value).astype(jnp.bfloat16)

    def plane_step(depth):
        plane = plane_variance(depth)
        return extended(plane, (("tile", 1),), 1)

    widened = lax.map(plane_step, jnp.arange(planes))
    padded = jnp.pad(stacked_columns_all(widened), ((1, 1), (0, 0), (0, 0), (0, 0)))
    result = stack_term(padded, weight_mats, 0, planes)[:, :, 0:strip_rows]
    result = result + stack_term(padded, weight_mats, 1, planes)[:, :, 1 : strip_rows + 1]
    result = result + stack_term(padded, weight_mats, 2, planes)[:, :, 2 : strip_rows + 2]
    return (result + conv_bias[None, :, None, None]).astype(jnp.bfloat16)


def solution(mesh):
    placed = (
        P("groups", "tile", None),
        P("groups", None, "tile", None),
        P("groups", None, "tile"),
        P("groups", None, "tile"),
        P("groups", None, None),
        P("groups", None, None),
        P(("groups", "tile")),
        P(),
        P(),
    )
    return jax.shard_map(
        on_device,
        mesh=mesh,
        in_specs=placed,
        out_specs=P("groups", None, "tile", None),
        check_vma=False,
    )
```

profile of v0, /device:TPU:24, one launch (start us, length us, event | category | flops | bytes accessed | tf_op | source)
XLA Modules:
  0.0 777.4 jit_solution(13067987021143764754)
XLA Ops:
  18.2 11.0 %collective-permute-done.2 = bf16[4,32,16,256]{3,2,1,0:T(8,128)(2,1)} collective-permute-done((bf16[4,32,16,256]{3,2,1,0:T(8,128)(2,1)}, bf16[4,32,16,256]{3,2,1,0:T(8,128)(2,1)}, u32[]{:S(2)}, u32[]{:S(2)}) %collective-permute-start.2) | collective-permute-done | bytes 1048608 | tf_op jit(solution)/shard_map/ppermute | solution.py:12
  30.5 8.8 %collective-permute-done.3 = bf16[4,32,16,256]{3,2,1,0:T(8,128)(2,1)} collective-permute-done((bf16[4,32,16,256]{3,2,1,0:T(8,128)(2,1)}, bf16[4,32,16,256]{3,2,1,0:T(8,128)(2,1)}, u32[]{:S(2)}, u32[]{:S(2)}) %collective-permute-start.3) | collective-permute-done | bytes 1048608 | tf_op jit(solution)/shard_map/ppermute | solution.py:12
  42.0 30.8 %collective-permute-done.5 = bf16[4,32,16,256]{3,2,1,0:T(8,128)(2,1)S(1)} collective-permute-done((bf16[4,32,16,256]{3,2,1,0:T(8,128)(2,1)}, bf16[4,32,16,256]{3,2,1,0:T(8,128)(2,1)S(1)}, u32[]{:S(2)}, u32[]{:S(2)}) %collective-permute-start.5) | collective-permute-done | bytes 1048608 | tf_op jit(solution)/shard_map/ppermute | solution.py:12
  75.2 555.3 %while.13 = (s32[]{:T(128)}, bf16[32,32,18,256]{3,1,2,0:T(8,128)(2,1)}, s32[32]{0:T(128)S(1)}, s32[4,32,16]{2,0,1:T(4,128)S(1)}, bf16[4,32,16]{2,0,1:T(4,128)(2,...) while((s32[]{:T(128)}, ...), condition=%wide.region_3.4_spmd.clone.clone, body=%wide.region_0.3_spmd.clone.clone.sunk | while | flops 357553216 | bytes 10070367 | solution.py:125
  79.2 3.9 fusion.57
  87.8 4.5 collective-permute-done.1
  97.3 3.9 fusion.57
  149.3 3.9 fusion.57
  183.9 3.9 fusion.57
  201.3 3.9 fusion.57
  218.6 3.9 fusion.57
  235.9 3.9 fusion.57
  253.2 3.9 fusion.57
  287.9 3.9 fusion.57
  305.3 3.9 fusion.57
  357.2 3.9 fusion.57
  374.5 3.9 fusion.57
  426.5 3.9 fusion.57
  495.9 3.9 fusion.57
  513.2 3.9 fusion.57
  547.9 3.9 fusion.57
  630.5 16.5 %pad_slice_fusion.1 = (bf16[32,32,18,256]{3,1,2,0:T(8,128)(2,1)}, bf16[32,32,18,256]{3,1,2,0:T(8,128)(2,1)}) fusion(bf16[32,32,18,256]{3,1,2,0:T(8,128)(2,1)} %get-tuple-element.153), kind=kLoop, calls=%fused_computation.47 | loop fusion | bytes 28311552 | tf_op jit(solution)/shard_map/slice | solution.py:32
  647.0 12.9 %fusion.43 = f32[32,18,256,8]{2,3,1,0:T(8,128)} fusion(bf16[3,3,8,96]{3,2,1,0:T(8,128)(2,1)S(1)} %reshape.21, bf16[32,32,18,256]{3,1,2,0:T(8,128)(2,1)} %get-tuple-element.295, bf16[32,32,18,256]{3,1,2,0:T(8,128)(2,1)} %get-tuple-element.153, bf16[32,32,18,256]{3,1,2,0:T(8,128)(2,1)} %get-tuple-element.294), kind=kOutput, calls=%fused_computation.76 | convolution fusion | flops 311427072 | bytes 33032192 | tf_op jit(solution)/shard_map/oc,pcrw->porw/dot_general | solution.py:45
  659.9 12.9 %fusion.41 = f32[32,18,256,8]{2,3,1,0:T(8,128)} fusion(bf16[3,3,8,96]{3,2,1,0:T(8,128)(2,1)S(1)} %reshape.21, bf16[32,32,18,256]{3,1,2,0:T(8,128)(2,1)} %get-tuple-element.295, bf16[32,32,18,256]{3,1,2,0:T(8,128)(2,1)} %get-tuple-element.153, bf16[32,32,18,256]{3,1,2,0:T(8,128)(2,1)} %get-tuple-element.294), kind=kOutput, calls=%fused_computation.71 | convolution fusion | flops 311427072 | bytes 33032192 | tf_op jit(solution)/shard_map/oc,pcrw->porw/dot_general | solution.py:45
  672.8 12.9 %fusion.39 = f32[32,18,256,8]{2,3,1,0:T(8,128)} fusion(bf16[3,3,8,96]{3,2,1,0:T(8,128)(2,1)S(1)} %reshape.21, bf16[32,32,18,256]{3,1,2,0:T(8,128)(2,1)} %get-tuple-element.295, bf16[32,32,18,256]{3,1,2,0:T(8,128)(2,1)} %get-tuple-element.153, bf16[32,32,18,256]{3,1,2,0:T(8,128)(2,1)} %get-tuple-element.294), kind=kOutput, calls=%fused_computation.66 | convolution fusion | flops 311427072 | bytes 33032192 | tf_op jit(solution)/shard_map/oc,pcrw->porw/dot_general | solution.py:45
  685.7 12.6 %fusion.44 = f32[32,18,256,8]{2,3,1,0:T(8,128)} fusion(bf16[3,3,8,96]{3,2,1,0:T(8,128)(2,1)S(1)} %reshape.21, bf16[32,32,18,256]{3,1,2,0:T(8,128)(2,1)} %get-tuple-element.295, bf16[32,32,18,256]{3,1,2,0:T(8,128)(2,1)} %get-tuple-element.153, bf16[32,32,18,256]{3,1,2,0:T(8,128)(2,1)} %get-tuple-element.294), kind=kOutput, calls=%fused_computation.78 | convolution fusion | flops 304349184 | bytes 33032192 | tf_op jit(solution)/shard_map/oc,pcrw->porw/dot_general | solution.py:38
  698.3 12.6 %fusion.42 = f32[32,18,256,8]{2,3,1,0:T(8,128)} fusion(bf16[3,3,8,96]{3,2,1,0:T(8,128)(2,1)S(1)} %reshape.21, bf16[32,32,18,256]{3,1,2,0:T(8,128)(2,1)} %get-tuple-element.295, bf16[32,32,18,256]{3,1,2,0:T(8,128)(2,1)} %get-tuple-element.153, bf16[32,32,18,256]{3,1,2,0:T(8,128)(2,1)} %get-tuple-element.294), kind=kOutput, calls=%fused_computation.73 | convolution fusion | flops 304349184 | bytes 33032192 | tf_op jit(solution)/shard_map/oc,pcrw->porw/dot_general | solution.py:38
  710.9 12.6 %fusion.40 = f32[32,18,256,8]{2,3,1,0:T(8,128)} fusion(bf16[3,3,8,96]{3,2,1,0:T(8,128)(2,1)S(1)} %reshape.21, bf16[32,32,18,256]{3,1,2,0:T(8,128)(2,1)} %get-tuple-element.295, bf16[32,32,18,256]{3,1,2,0:T(8,128)(2,1)} %get-tuple-element.153, bf16[32,32,18,256]{3,1,2,0:T(8,128)(2,1)} %get-tuple-element.294), kind=kOutput, calls=%fused_computation.68 | convolution fusion | flops 304349184 | bytes 33032192 | tf_op jit(solution)/shard_map/oc,pcrw->porw/dot_general | solution.py:38
  723.5 15.3 %add_bitcast_fusion.3 = f32[32,8,18,256]{3,1,2,0:T(8,128)} fusion(f32[32,18,256,8]{2,3,1,0:T(8,128)} %fusion.44, f32[32,18,256,8]{2,3,1,0:T(8,128)} %fusion.43, bf16[3,3,8,96]{3,2,1,0:T(8,128)(2,1)S(1)} %reshape.21, bf16[32,32,18,256]{3,1,2,0:T(8,128)(2,1)} %get-tuple-element.295, bf16[32,32,18,256]{3,1,2,0:T(8,128)(2,1)} %get-tuple-element.153, ...), kind=kOutput, calls=%fused_computation.50 | convolution fusion | flops 306708480 | bytes 42469376 | tf_op jit(solution)/shard_map/oc,pcrw->porw/dot_general | solution.py:45
  738.8 15.2 %add_bitcast_fusion.2 = f32[32,8,18,256]{3,1,2,0:T(8,128)} fusion(f32[32,18,256,8]{2,3,1,0:T(8,128)} %fusion.42, f32[32,18,256,8]{2,3,1,0:T(8,128)} %fusion.41, bf16[3,3,8,96]{3,2,1,0:T(8,128)(2,1)S(1)} %reshape.21, bf16[32,32,18,256]{3,1,2,0:T(8,128)(2,1)} %get-tuple-element.295, bf16[32,32,18,256]{3,1,2,0:T(8,128)(2,1)} %get-tuple-element.153, ...), kind=kOutput, calls=%fused_computation.49 | convolution fusion | flops 306708480 | bytes 42469376 | tf_op jit(solution)/shard_map/oc,pcrw->porw/dot_general | solution.py:45
  754.0 15.3 %add_bitcast_fusion.1 = f32[32,8,18,256]{3,1,2,0:T(8,128)} fusion(f32[32,18,256,8]{2,3,1,0:T(8,128)} %fusion.40, f32[32,18,256,8]{2,3,1,0:T(8,128)} %fusion.39, bf16[3,3,8,96]{3,2,1,0:T(8,128)(2,1)S(1)} %reshape.21, bf16[32,32,18,256]{3,1,2,0:T(8,128)(2,1)} %get-tuple-element.295, bf16[32,32,18,256]{3,1,2,0:T(8,128)(2,1)} %get-tuple-element.153, ...), kind=kOutput, calls=%fused_computation.48 | convolution fusion | flops 306708480 | bytes 42469376 | tf_op jit(solution)/shard_map/oc,pcrw->porw/dot_general | solution.py:45
  769.3 6.1 fusion.38
  (522 shorter events, 449.6 us)
Async XLA Ops:
  0.0 29.2 %collective-permute-start.2 = (bf16[4,32,16,256]{3,2,1,0:T(8,128)(2,1)}, bf16[4,32,16,256]{3,2,1,0:T(8,128)(2,1)}, u32[]{:S(2)}, u32[]{:S(2)}) collective-permute-start(bf16[4,32,16,256]{3,2,1,0:T(8,128)(2,1)} %param.12), channel_id=1, source_target_pairs={{0,2},{1,3},{2,4},{3,5},{4,6},{5,7},{6,8},{7,9},{8,10},{9,11},{10,... | collective-permute-start | bytes 3145736 | tf_op jit(solution)/shard_map/ppermute | solution.py:12
  3.4 38.5 %collective-permute-start.4 = (bf16[4,32,16,256]{3,2,1,0:T(8,128)(2,1)}, bf16[4,32,16,256]{3,2,1,0:T(8,128)(2,1)S(1)}, u32[]{:S(2)}, u32[]{:S(2)}) collective-permute-start(bf16[4,32,16,256]{3,2,1,0:T(8,128)(2,1)} %param.12), channel_id=1, source_target_pairs={{1,0},{2,1},{3,2},{4,3},{5,4},{6,5},{7,6},{8,7},{9,8},{10,9},{11,1... | collective-permute-start | bytes 3145736 | tf_op jit(solution)/shard_map/ppermute | solution.py:12
  5.9 33.4 %collective-permute-start.3 = (bf16[4,32,16,256]{3,2,1,0:T(8,128)(2,1)}, bf16[4,32,16,256]{3,2,1,0:T(8,128)(2,1)}, u32[]{:S(2)}, u32[]{:S(2)}) collective-permute-start(bf16[4,32,16,256]{3,2,1,0:T(8,128)(2,1)} %param.12), channel_id=1, source_target_pairs={{0,1},{1,2},{2,3},{3,4},{4,5},{5,6},{6,7},{7,8},{8,9},{9,10},{10,1... | collective-permute-start | bytes 3145736 | tf_op jit(solution)/shard_map/ppermute | solution.py:12
  7.8 65.0 %collective-permute-start.5 = (bf16[4,32,16,256]{3,2,1,0:T(8,128)(2,1)}, bf16[4,32,16,256]{3,2,1,0:T(8,128)(2,1)S(1)}, u32[]{:S(2)}, u32[]{:S(2)}) collective-permute-start(bf16[4,32,16,256]{3,2,1,0:T(8,128)(2,1)} %param.12), channel_id=1, source_target_pairs={{2,0},{3,1},{4,2},{5,3},{6,4},{7,5},{8,6},{9,7},{10,8},{11,9},{12,... | collective-permute-start | bytes 3145736 | tf_op jit(solution)/shard_map/ppermute | solution.py:12
  85.4 6.9 collective-permute-start.1
  103.5 6.1 collective-permute-start.1
  120.8 6.1 collective-permute-start.1
  138.1 6.1 collective-permute-start.1
  155.5 6.1 collective-permute-start.1
  172.8 6.1 collective-permute-start.1
  190.1 6.1 collective-permute-start.1
  207.4 6.1 collective-permute-start.1
  224.7 6.1 collective-permute-start.1
  242.0 6.1 collective-permute-start.1
  259.4 6.1 collective-permute-start.1
  276.7 6.1 collective-permute-start.1
  294.1 6.1 collective-permute-start.1
  311.4 6.1 collective-permute-start.1
  328.7 6.1 collective-permute-start.1
  346.0 6.1 collective-permute-start.1
  363.3 6.1 collective-permute-start.1
  415.3 6.1 collective-permute-start.1
  432.7 6.1 collective-permute-start.1
  467.4 6.1 collective-permute-start.1
  484.7 6.1 collective-permute-start.1
  502.0 6.1 collective-permute-start.1
  519.4 6.1 collective-permute-start.1
  536.7 6.1 collective-permute-start.1
  554.0 6.1 collective-permute-start.1
  571.3 6.1 collective-permute-start.1
  588.7 6.1 collective-permute-start.1
  623.3 6.1 collective-permute-start.1
  (38 other events, 181.2 us)
where the time goes:
time: 784 us; the launch traced here: 777 us
  matrix products  246 us (31%)
  waiting for transfers between devices  170 us (22%)
  starting transfers between devices  150 us (19%)
  local copies, waits for them, and re-layouts  99.4 us (13%)
  loops' own time  65 us (8%)
  other arithmetic  46.2 us (6%)
    dot_general x32, matrix products, plane_variance(): jnp.einsum('vcrw,vwk->vcrk', rowmix, col_matrix, preferred_element_type=j...  124 us
    ppermute x32, waiting for transfers between devices, extended(): lax.ppermute(lax.slice_in_dim(block, block.shape[dim] - width, None, axis...  119 us
    dot_general x6, matrix products, stack_term(): jnp.einsum('oc,pcrw->porw', weight_mats[depth_tap, offset], padded[depth_...  84.5 us
    ppermute x32, starting transfers between devices, extended(): lax.ppermute(lax.slice_in_dim(block, block.shape[dim] - width, None, axis...  77 us
    another operation x1, loops' own time, on_device(): widened = lax.map(plane_step, jnp.arange(planes))  65 us
    ppermute x32, starting transfers between devices, extended(): lax.ppermute(lax.slice_in_dim(block, 0, width, axis=dim), axis, backward)  61.5 us
    ppermute x4, waiting for transfers between devices, shifted(): return lax.ppermute(x, axis, pairs)  50.6 us
    dot_general x3, matrix products, stack_term(): jnp.einsum('oc,pcrw->porw', weight_mats[0, offset], padded[0:planes], pre...  37.8 us
  transfers between devices with their start and end apart: 68, of which 35 were waited for; matrix products, arithmetic and copies ran while one was open for 1% of the time, Pallas kernels for 0%

commit v1 on v0

v1 whole, which is shorter than its diff:
```python
import jax
import jax.numpy as jnp
from jax import lax
from jax.experimental import pallas as pl
from jax.experimental.pallas import tpu as pltpu
from jax.sharding import PartitionSpec as P

VMEM_LIMIT = 56 * 1024 * 1024
CHUNKS = (16, 16)
LANES = 128


def routed(x, target):
    length = lax.axis_size("tile")
    pairs = [(i, target(i)) for i in range(length) if 0 <= target(i) < length]
    return lax.ppermute(x, "tile", pairs)


def onward(i):
    return i + 4 if i % 4 < 2 else i - 4


def gathered(block):
    across = routed(block, lambda i: i ^ 2)
    beside = routed(block, lambda i: i ^ 1)
    along = routed(across, onward)
    return [
        block,
        beside,
        across,
        routed(across, lambda i: i ^ 1),
        along,
        routed(along, lambda i: i ^ 1),
    ]


def strip_offsets(tile):
    low = (tile % 4) < 2
    across = jnp.where(low, 2, -2)
    along = -across
    beside = jnp.where(tile % 2 == 0, 1, -1)
    return jnp.stack([tile, tile + beside, tile + across, tile + beside + across, tile + along, tile + beside + along])


def warp_kernel(strips, views, planes, chans, rows, cols, *refs):
    inv_ref, refs = refs[0], refs[1:]
    strip_refs, refs = refs[:strips], refs[strips:]
    base_ref, rowmat_ref, tap_ref, frac_ref, var_ref, edge_ref, rowmix = refs
    count = chans * rows
    half = rows // 2

    def mix_rows(c, _):
        for v in range(views):
            band = jnp.concatenate([s[v, c] for s in strip_refs], axis=0)
            mixed = jnp.dot(rowmat_ref[v], band, preferred_element_type=jnp.float32)
            rowmix[v, :, pl.ds(pl.multiple_of(c * rows, rows), rows), :] = mixed.astype(jnp.bfloat16).reshape(
                planes, rows, cols
            )
        return 0

    lax.fori_loop(0, chans, mix_rows, 0)
    inv = inv_ref[0, 0]
    index = lax.broadcasted_iota(jnp.int32, (cols, cols), 0).astype(jnp.bfloat16)

    def plane(d, _):
        base = base_ref[...].reshape(count, cols).astype(jnp.float32)
        total = base
        squares = base * base
        for v in range(views):
            tap = tap_ref[v, pl.ds(d, 1), :].astype(jnp.float32)
            frac = frac_ref[v, pl.ds(d, 1), :]
            mat = jnp.where(
                index == tap.astype(jnp.bfloat16),
                (1.0 - frac).astype(jnp.bfloat16),
                jnp.where(
                    index == (tap + 1.0).astype(jnp.bfloat16), frac.astype(jnp.bfloat16), jnp.zeros((), jnp.bfloat16)
                ),
            )
            warped = jnp.dot(rowmix[v, d], mat, preferred_element_type=jnp.float32)
            total = total + warped
            squares = squares + warped * warped
        mean = total * inv
        var = (squares * inv - mean * mean).reshape(chans, 2, half, cols)
        for h in range(2):
            var_ref[d, h] = var[:, h].reshape(chans * half, cols).astype(jnp.bfloat16)
            edge_ref[h, d] = var[:, h, h * (half - 1)].astype(jnp.bfloat16)
        return 0

    lax.fori_loop(0, planes, plane, 0)


def warp(inv, strips, base, rowmat, tap, frac):
    views, chans, rows, cols = strips[0].shape
    planes = tap.shape[1]
    vmem = pl.BlockSpec(memory_space=pltpu.VMEM)

    def kernel(*refs):
        warp_kernel(len(strips), views, planes, chans, rows, cols, *refs)

    return pl.pallas_call(
        kernel,
        out_shape=(
            jax.ShapeDtypeStruct((planes, 2, chans * rows // 2, cols), jnp.bfloat16),
            jax.ShapeDtypeStruct((2, planes, chans, cols), jnp.bfloat16),
        ),
        in_specs=[pl.BlockSpec(memory_space=pltpu.SMEM)] + [vmem] * (len(strips) + 4),
        out_specs=(vmem, vmem),
        scratch_shapes=[pltpu.VMEM((views, planes, chans * rows, cols), jnp.bfloat16)],
        compiler_params=pltpu.CompilerParams(vmem_limit_bytes=VMEM_LIMIT),
        cost_estimate=pl.CostEstimate(
            flops=2 * views * planes * chans * rows * cols * cols * 2, bytes_accessed=4 << 20, transcendentals=0
        ),
        name="warp",
    )(inv, *strips, base, rowmat, tap, frac)


def joined_columns(parts):
    left, middle, right = parts
    cols = middle.shape[-1]
    lane = lax.broadcasted_iota(jnp.int32, middle.shape, middle.ndim - 1)
    left = jnp.where(lane == 0, 0.0, pltpu.roll(left, 1, middle.ndim - 1))
    right = jnp.where(lane == cols - 1, 0.0, pltpu.roll(right, cols - 1, middle.ndim - 1))
    return middle + left + right


def edge_kernel(planes, group, outs, cols, nchunks, *refs):
    edge_refs, (mat_ref, up_ref, down_ref, acc) = refs[:nchunks], refs[nchunks:]
    for side, out in ((0, up_ref), (1, down_ref)):
        acc[...] = jnp.zeros_like(acc)
        for start in range(0, planes, group):
            terms = jnp.zeros((3 * (group + 2) * outs, cols), jnp.float32)
            offset = 0
            for edge in edge_refs:
                chans = edge.shape[2]
                rhs = edge[side, start : start + group].reshape(group * chans, cols)
                lhs = mat_ref[side, :, offset * group : (offset + chans) * group]
                terms = terms + jnp.dot(lhs, rhs, preferred_element_type=jnp.float32)
                offset += chans
            rows = (group + 2) * outs
            acc[start * outs : start * outs + rows] += joined_columns([terms[e * rows : (e + 1) * rows] for e in range(3)])
        out[...] = acc[outs : outs + planes * outs].astype(jnp.bfloat16)


def edge_terms(edges, mat, outs):
    planes, cols = edges[0].shape[1], edges[0].shape[3]
    group = mat.shape[1] // (3 * outs) - 2
    vmem = pl.BlockSpec(memory_space=pltpu.VMEM)

    def kernel(*refs):
        edge_kernel(planes, group, outs, cols, len(edges), *refs)

    shape = jax.ShapeDtypeStruct((planes * outs, cols), jnp.bfloat16)
    return pl.pallas_call(
        kernel,
        out_shape=(shape, shape),
        in_specs=[vmem] * (len(edges) + 1),
        out_specs=(vmem, vmem),
        scratch_shapes=[pltpu.VMEM(((planes + 2) * outs, cols), jnp.float32)],
        compiler_params=pltpu.CompilerParams(vmem_limit_bytes=VMEM_LIMIT),
        name="edge",
    )(*edges, mat)


def filter_kernel(planes, rows, outs, cols, nchunks, *refs):
    bias_ref, refs = refs[0], refs[1:]
    var_refs, (mat_ref, above_ref, below_ref, out_ref, flat) = refs[:nchunks], refs[nchunks:]
    half = rows // 2
    depth = mat_ref.shape[2] // 3
    width = (half + 1) * outs

    def plane(d, taps):
        parts = []
        for h in range(2):
            rhs = jnp.concatenate([v[d + a - 1, h] for a in taps for v in var_refs], axis=0)
            lhs = mat_ref[h, :, taps[0] * depth : (taps[-1] + 1) * depth]
            terms = jnp.dot(lhs, rhs, preferred_element_type=jnp.float32)
            parts.append(joined_columns([terms[e * width : (e + 1) * width] for e in range(3)]))
        upper, lower = parts
        at = pl.multiple_of(d * outs, outs)
        upper = upper + jnp.concatenate([above_ref[pl.ds(at, outs), :].astype(jnp.float32), jnp.zeros((half * outs, cols))])
        lower = lower + jnp.concatenate([jnp.zeros((half * outs, cols)), below_ref[pl.ds(at, outs), :].astype(jnp.float32)])
        whole = jnp.concatenate(
            [
                upper[: (half - 1) * outs],
                upper[(half - 1) * outs :] + lower[: 2 * outs],
                lower[2 * outs :],
            ]
        )
        for lane in range(cols // LANES):
            lanes = slice(lane * LANES, (lane + 1) * LANES)
            flat[lane] = whole[:, lanes]
            for o in range(outs):
                out_ref[d, o, :, lanes] = (flat[lane, pl.ds(o, rows, stride=outs), :] + bias_ref[0, o]).astype(jnp.bfloat16)

    plane(0, (1, 2))

    def inner(d, _):
        plane(d, (0, 1, 2))
        return 0

    lax.fori_loop(1, planes - 1, inner, 0)
    plane(planes - 1, (0, 1))


def filtered(bias, variances, mat, above, below, rows, outs):
    planes, _, _, cols = variances[0].shape
    vmem = pl.BlockSpec(memory_space=pltpu.VMEM)

    def kernel(*refs):
        filter_kernel(planes, rows, outs, cols, len(variances), *refs)

    return pl.pallas_call(
        kernel,
        out_shape=jax.ShapeDtypeStruct((planes, outs, rows, cols), jnp.bfloat16),
        in_specs=[pl.BlockSpec(memory_space=pltpu.SMEM)] + [vmem] * (len(variances) + 3),
        out_specs=vmem,
        scratch_shapes=[pltpu.VMEM((cols // LANES, rows * outs, LANES), jnp.float32)],
        compiler_params=pltpu.CompilerParams(vmem_limit_bytes=VMEM_LIMIT),
        name="filter",
    )(bias, *variances, mat, above, below)


def filter_matrix(weight, half):
    outs, chans = weight.shape[3:]
    mats = []
    for h in range(2):
        target = jnp.arange(half + 1) - h
        tap = jnp.arange(half)[None, :] - target[:, None] + 1
        pick = (tap[:, :, None] == jnp.arange(3)).astype(weight.dtype)
        mats.append(jnp.einsum("grb,abeoc->egoacr", pick, weight).reshape(3 * (half + 1) * outs, 3 * chans * half))
    return jnp.stack(mats)


def edge_matrix(weight, chunks, group):
    outs, chans = weight.shape[3:]
    tap = jnp.arange(group)[None, :] - jnp.arange(group + 2)[:, None] + 2
    pick = (tap[:, :, None] == jnp.arange(3)).astype(weight.dtype)
    sides = []
    for b in (2, 0):
        parts = []
        offset = 0
        for size in chunks:
            part = weight[:, b, :, :, offset : offset + size]
            parts.append(jnp.einsum("pqa,aeoc->epoqc", pick, part).reshape(3 * (group + 2) * outs, group * size))
            offset += size
        sides.append(jnp.concatenate(parts, axis=1))
    return jnp.stack(sides)


def on_device(
    ref_feat, src_feat, row_tap, row_frac, col_tap, col_frac, view_count, conv_weight, conv_bias
):
    rows = ref_feat.shape[1]
    views = src_feat.shape[0]
    planes = row_tap.shape[1]
    outs = conv_weight.shape[3]
    tile = lax.axis_index("tile")

    starts = strip_offsets(tile) * rows
    index = (starts[:, None] + jnp.arange(rows)).reshape(-1)
    keep = (1.0 - row_frac.astype(jnp.float32)).astype(jnp.bfloat16)
    valid = (jnp.arange(views) < view_count[0])[:, None, None, None]
    zero = jnp.zeros((), jnp.bfloat16)
    rowmat = jnp.where(
        (index == row_tap[..., None]) & valid,
        keep[..., None],
        jnp.where((index == row_tap[..., None] + 1) & valid, row_frac[..., None], zero),
    ).reshape(views, planes * rows, -1)
    inv = (1.0 / (1.0 + view_count.astype(jnp.float32))).reshape(1, 1)
    frac = col_frac.astype(jnp.float32)
    filter_mat = filter_matrix(conv_weight, rows // 2)
    edge_mat = edge_matrix(conv_weight, CHUNKS, 8)

    variances = []
    edges = []
    offset = 0
    for size in CHUNKS:
        strips = gathered(src_feat[:, offset : offset + size])
        var, edge = warp(inv, strips, ref_feat[offset : offset + size], rowmat, col_tap, frac)
        variances.append(var)
        edges.append(edge)
        offset += size
    up, down = edge_terms(edges, edge_mat, outs)
    above = routed(down, lambda i: i + 1)
    below = routed(up, lambda i: i - 1)
    return filtered(conv_bias.reshape(1, -1), variances, filter_mat, above, below, rows, outs)


def solution(mesh):
    placed = (
        P("groups", "tile", None),
        P("groups", None, "tile", None),
        P("groups", None, "tile"),
        P("groups", None, "tile"),
        P("groups", None, None),
        P("groups", None, None),
        P(("groups", "tile")),
        P(),
        P(),
    )
    return jax.shard_map(
        on_device,
        mesh=mesh,
        in_specs=placed,
        out_specs=P("groups", None, "tile", None),
        check_vma=False,
    )
```

time: 784 us -> 150 us (0.19)
  matrix products: 246 us -> 5.2 us
  waiting for transfers between devices: 170 us -> 19.2 us
  starting transfers between devices: 150 us -> 12.1 us
  Pallas kernels: 0 us -> 69.2 us
  loops' own time: 65 us -> 0 us
  local copies, waits for them, and re-layouts: 99.4 us -> 36.4 us
  other arithmetic: 46.2 us -> 6.23 us
    dot_general x41 -> x6, matrix products: 246 us -> 5.2 us  [the longest x2 3.37 us: filter_matrix(): jnp.einsum('grb,abeoc->egoacr', pick, weight)]
    ppermute x68 -> x12, waiting for transfers between devices: 170 us -> 19.2 us  [routed(): return lax.ppermute(x, 'tile', pairs)]
    ppermute x68 -> x12, starting transfers between devices: 150 us -> 12.1 us  [routed(): return lax.ppermute(x, 'tile', pairs)]
    pallas_call x0 -> x4, Pallas kernels: none -> 69.2 us  [the longest x2 47 us: warp(): pl.pallas_call(kernel, out_shape=(jax.ShapeDtypeStruct((planes, 2, chans...]
    another operation x1 -> x0, loops' own time: 65 us -> none  [on_device(): widened = lax.map(plane_step, jnp.arange(planes))]
    dynamic_slice x64 -> x0, local copies, waits for them, and re-layouts: 43.3 us -> none  [the longest x32 24.6 us: plane_variance(): col_taps = lax.dynamic_index_in_dim(col_tap, depth, 1, keepdims=False)]
    convert_element_type x68 -> x2, other arithmetic: 37.1 us -> 1.38 us  [the longest x1 0.72 us: on_device(): keep = (1.0 - row_frac.astype(jnp.float32)).astype(jnp.bfloat16)]
    dynamic_update_slice x32 -> x0, local copies, waits for them, and re-layouts: 25.3 us -> none  [on_device(): widened = lax.map(plane_step, jnp.arange(planes))]
  transfers between devices with their start and end apart: 68 -> 12, of which waited for: 35 -> 4; matrix products, arithmetic and copies ran while one was open for 1% -> 29% of each run, Pallas kernels for 0% -> 16%
where the time goes in v1:
time: 150 us; the launch traced here: 149 us
  Pallas kernels  69.2 us (46%)
  local copies, waits for them, and re-layouts  36.4 us (24%)
  waiting for transfers between devices  19.2 us (13%)
  starting transfers between devices  12.1 us (8%)
  other arithmetic  6.23 us (4%)
  matrix products  5.2 us (3%)
    pallas_call x2, Pallas kernels, warp(): pl.pallas_call(kernel, out_shape=(jax.ShapeDtypeStruct((planes, 2, chans...  47 us
    pallas_call x1, Pallas kernels, filtered(): pl.pallas_call(kernel, out_shape=jax.ShapeDtypeStruct((planes, outs, rows...  19.5 us
    ppermute x12, waiting for transfers between devices, routed(): return lax.ppermute(x, 'tile', pairs)  19.2 us
    another operation x2, local copies, waits for them, and re-layouts, filter_matrix(): return jnp.stack(mats)  16.2 us
    ppermute x12, starting transfers between devices, routed(): return lax.ppermute(x, 'tile', pairs)  12.1 us
    transpose x2, local copies, waits for them, and re-layouts, filter_matrix(): jnp.einsum('grb,abeoc->egoacr', pick, weight)  9.32 us
    dot_general x2, matrix products, filter_matrix(): jnp.einsum('grb,abeoc->egoacr', pick, weight)  3.37 us
  transfers between devices with their start and end apart: 12, of which 4 were waited for; matrix products, arithmetic and copies ran while one was open for 29% of the time, Pallas kernels for 16%

profile of v1, /device:TPU:24, one launch (start us, length us, event | category | flops | bytes accessed | tf_op | source)
XLA Modules:
  0.0 149.2 jit_solution(5610602195950322660)
XLA Ops:
  0.0 2.3 %fusion.15 = (bf16[4,16,16,256]{3,2,1,0:T(8,128)(2,1)}, bf16[4,16,16,256]{3,2,1,0:T(8,128)(2,1)}) fusion(bf16[4,32,16,256]{3,2,1,0:T(8,128)(2,1)} %param.10), kind=kLoop, calls=%fused_computation.37 | loop fusion | bytes 2097152 | tf_op jit(solution)/shard_map/slice | solution.py:278
  2.3 1.5 %collective-permute-start.6 = (bf16[4,16,16,256]{3,2,1,0:T(8,128)(2,1)}, bf16[4,16,16,256]{3,2,1,0:T(8,128)(2,1)}, u32[]{:S(2)}, u32[]{:S(2)}) collective-permute-start(bf16[4,16,16,256]{3,2,1,0:T(8,128)(2,1)} %get-tuple-element.17.refs_1_), channel_id=1, source_target_pairs={{0,2},{1,3},{2,0},{3,1},{4,6},{5,7},{6,4},{7,5},{8,10},{9,11},{10,... | collective-permute-start | bytes 1572872 | tf_op jit(solution)/shard_map/ppermute | solution.py:16
  4.6 0.8 broadcast_add_fusion
  5.4 0.7 subtract_convert_fusion
  6.1 0.9 fusion.17
  10.3 1.1 copy.31
  11.4 1.4 reshape.152
  14.9 0.7 pad_maximum_fusion.1.refs_2_
  15.6 1.8 %collective-permute-done.6.refs_3_ = bf16[4,16,16,256]{3,2,1,0:T(8,128)(2,1)} collective-permute-done((bf16[4,16,16,256]{3,2,1,0:T(8,128)(2,1)}, bf16[4,16,16,256]{3,2,1,0:T(8,128)(2,1)}, u32[]{:S(2)}, u32[]{:S(2)}) %collective-permute-start.6) | collective-permute-done | bytes 524320 | tf_op jit(solution)/shard_map/ppermute | solution.py:16
  17.4 1.3 collective-permute-start.8
  18.7 0.7 fusion.16
  19.4 8.0 %collective-permute-done.1.refs_3_ = bf16[4,16,16,256]{3,2,1,0:T(8,128)(2,1)} collective-permute-done((bf16[4,16,16,256]{3,2,1,0:T(8,128)(2,1)}, bf16[4,16,16,256]{3,2,1,0:T(8,128)(2,1)}, u32[]{:S(2)}, u32[]{:S(2)}) %collective-permute-start.1) | collective-permute-done | bytes 524320 | tf_op jit(solution)/shard_map/ppermute | solution.py:16
  27.5 1.3 collective-permute-start.3
  28.8 3.7 %collective-permute-done.8.refs_5_ = bf16[4,16,16,256]{3,2,1,0:T(8,128)(2,1)} collective-permute-done((bf16[4,16,16,256]{3,2,1,0:T(8,128)(2,1)}, bf16[4,16,16,256]{3,2,1,0:T(8,128)(2,1)}, u32[]{:S(2)}, u32[]{:S(2)}) %collective-permute-start.8) | collective-permute-done | bytes 524320 | tf_op jit(solution)/shard_map/ppermute | solution.py:16
  32.7 0.7 convert_element_type.18.refs_10_
  33.3 2.3 %and_select_fusion.1.refs_8_ = bf16[4,512,96]{2,1,0:T(8,128)(2,1)} fusion(s32[4,512]{1,0:T(4,128)S(1)} %eq.98, s32[4,512]{1,0:T(4,128)S(1)} %eq.95, s32[96]{0:T(128)S(1)} %add.100, pred[4]{0:T(512)(128)(4,1)S(1)} %iota_compare_fusion.3, bf16[4,512]{1,0:T(4,128)(2,1)S(1)} %broadcast_in_dim.26, bf16[4,512]{1,0:T(4,128)(2,1)S(1)} %broadcast_in_dim.24), kind=kLoop, calls=%fused_computation.7 | loop fusion | flops 1179648 | bytes 418180 | tf_op jit(solution)/shard_map/jit(_where)/select_n | solution.py:264
  35.7 1.1 convolution_bitcast_fusion
  37.4 5.6 %collective-permute-done.3.refs_5_ = bf16[4,16,16,256]{3,2,1,0:T(8,128)(2,1)S(1)} collective-permute-done((bf16[4,16,16,256]{3,2,1,0:T(8,128)(2,1)}, bf16[4,16,16,256]{3,2,1,0:T(8,128)(2,1)S(1)}, u32[]{:S(2)}, u32[]{:S(2)}) %collective-permute-start.3) | collective-permute-done | bytes 524320 | tf_op jit(solution)/shard_map/ppermute | solution.py:16
  43.1 23.6 %warp.3 = (bf16[32,2,128,256]{3,2,1,0:T(8,128)(2,1)}, bf16[2,32,16,256]{3,2,1,0:T(8,128)(2,1)}) custom-call(f32[1,1]{1,0:T(1,128)} %bitcast.1.refs_0_, bf16[4,16,16,256]{3,2,1,0:T(8,128)(2,1)} %get-tuple-element.17.refs_1_, bf16[4,16,16,256]{3,2,1,0:T(8,128)(2,1)} %collective-permute-done.5.refs_2_, bf16[4,16,16,256]{3,2,1,0:T(8,128)(2,1)} %collective-permute-done.6.refs_3_, ...), custom_call_target="tpu_custom_call" | custom-call | flops 8589934592 | bytes 4194304 | tf_op jit(solution)/shard_map/warp/pallas_call | solution.py:100
  66.7 0.8 copy-done.9
  67.7 23.4 %warp.2 = (bf16[32,2,128,256]{3,2,1,0:T(8,128)(2,1)}, bf16[2,32,16,256]{3,2,1,0:T(8,128)(2,1)}) custom-call(f32[1,1]{1,0:T(1,128)} %bitcast.1.refs_0_, bf16[4,16,16,256]{3,2,1,0:T(8,128)(2,1)} %get-tuple-element.18.refs_1_, bf16[4,16,16,256]{3,2,1,0:T(8,128)(2,1)} %collective-permute-done.refs_2_, bf16[4,16,16,256]{3,2,1,0:T(8,128)(2,1)} %collective-permute-done.1.refs_3_, ...), custom_call_target="tpu_custom_call" | custom-call | flops 8589934592 | bytes 4194304 | tf_op jit(solution)/shard_map/warp/pallas_call | solution.py:100
  91.1 2.7 %edge.1 = (bf16[256,256]{1,0:T(8,128)(2,1)}, bf16[256,256]{1,0:T(8,128)(2,1)}) custom-call(bf16[2,32,16,256]{3,2,1,0:T(8,128)(2,1)} %get-tuple-element.13.refs_0_, bf16[2,32,16,256]{3,2,1,0:T(8,128)(2,1)} %get-tuple-element.14.refs_1_, bf16[2,240,256]{2,1,0:T(8,128)(2,1)} %pad_maximum_fusion.1.refs_2_), custom_call_target="tpu_custom_call" | custom-call | tf_op jit(solution)/shard_map/edge/pallas_call | solution.py:153
  93.7 2.2 %collective-permute-start.10 = (bf16[256,256]{1,0:T(8,128)(2,1)}, bf16[256,256]{1,0:T(8,128)(2,1)S(1)}, u32[]{:S(2)}, u32[]{:S(2)}) collective-permute-start(bf16[256,256]{1,0:T(8,128)(2,1)} %get-tuple-element.15), channel_id=1, source_target_pairs={{0,1},{1,2},{2,3},{3,4},{4,5},{5,6},{6,7},{7,8},{8,9},{9,10},{10,1... | collective-permute-start | bytes 393224 | tf_op jit(solution)/shard_map/ppermute | solution.py:16
  96.0 4.4 %collective-permute-start.11 = (bf16[256,256]{1,0:T(8,128)(2,1)}, bf16[256,256]{1,0:T(8,128)(2,1)S(1)}, u32[]{:S(2)}, u32[]{:S(2)}) collective-permute-start(bf16[256,256]{1,0:T(8,128)(2,1)} %get-tuple-element.16), channel_id=1, source_target_pairs={{1,0},{2,1},{3,2},{4,3},{5,4},{6,5},{7,6},{8,7},{9,8},{10,9},{11,1... | collective-permute-start | bytes 393224 | tf_op jit(solution)/shard_map/ppermute | solution.py:16
  100.4 2.2 %convolution_bitcast_fusion.1 = bf16[3,9,8,3,32,8]{4,1,2,0,3,5:T(8,128)(2,1)} fusion(bf16[3,3,3,8,32]{4,3,2,1,0:T(8,128)(2,1)S(1)} %copy-done.1, s32[9,8]{0,1:T(8,128)S(1)} %subtract_add_fusion.2), kind=kOutput, calls=%fused_computation.1 | convolution fusion | flops 995544 | bytes 345888 | tf_op jit(solution)/shard_map/grb,abeoc->egoacr/dot_general | solution.py:230
  102.6 4.7 %copy.29 = bf16[3,9,8,3,32,8]{5,4,3,2,1,0:T(8,128)(2,1)} copy(bf16[3,9,8,3,32,8]{4,1,2,0,3,5:T(8,128)(2,1)S(1)} %convolution_bitcast_fusion) | data formatting | bytes 663552 | tf_op jit(solution)/shard_map/grb,abeoc->egoacr/transpose | solution.py:230
  107.3 8.2 %stack_reshape.7 = bf16[1,216,768]{2,1,0:T(8,128)(2,1)S(1)} reshape(bf16[3,9,8,3,32,8]{5,4,3,2,1,0:T(8,128)(2,1)} %copy.29) | data formatting | bytes 663552 | tf_op jit(solution)/shard_map/stack;reshape | solution.py:231
  115.5 4.7 %copy.27 = bf16[3,9,8,3,32,8]{5,4,3,2,1,0:T(8,128)(2,1)} copy(bf16[3,9,8,3,32,8]{4,1,2,0,3,5:T(8,128)(2,1)S(1)} %copy-done) | data formatting | bytes 663552 | tf_op jit(solution)/shard_map/grb,abeoc->egoacr/transpose | solution.py:230
  120.1 8.0 %stack_reshape.6 = bf16[1,216,768]{2,1,0:T(8,128)(2,1)S(1)} reshape(bf16[3,9,8,3,32,8]{5,4,3,2,1,0:T(8,128)(2,1)} %copy.27) | data formatting | bytes 663552 | tf_op jit(solution)/shard_map/stack;reshape | solution.py:231
  128.1 0.9 pad_maximum_fusion.refs_3_
  129.1 0.6 copy-done.3
  129.8 19.5 %filter.1 = bf16[32,8,16,256]{3,2,1,0:T(8,128)(2,1)} custom-call(f32[1,8]{1,0:T(1,128)} %bitcast.78, bf16[32,2,128,256]{3,2,1,0:T(8,128)(2,1)} %get-tuple-element.11.refs_1_, bf16[32,2,128,256]{3,2,1,0:T(8,128)(2,1)} %get-tuple-element.12.refs_2_, bf16[2,216,768]{2,1,0:T(8,128)(2,1)} %pad_maximum_fusion.refs_3_, bf16[256,256]{1,0:T(8,128)(2,1)} %copy-done.3, ...), custom_call_target="tpu_custom_call" | custom-call | tf_op jit(solution)/shard_map/filter/pallas_call | solution.py:212
  (63 shorter events, 6.5 us)
Async XLA Ops:
  0.0 8.9 %copy-start.5 = (s32[4,32,16]{1,2,0:T(8,128)S(1)}, s32[4,32,16]{1,2,0:T(8,128)}, u32[]{:S(2)}) copy-start(s32[4,32,16]{1,2,0:T(8,128)} %param.11) | copy-start | bytes 24580
  2.3 6.7 %copy-start.7 = (bf16[4,32,16]{1,2,0:T(8,128)(2,1)S(1)}, bf16[4,32,16]{1,2,0:T(8,128)(2,1)}, u32[]{:S(2)}) copy-start(bf16[4,32,16]{1,2,0:T(8,128)(2,1)} %param.12) | copy-start | bytes 12292
  2.3 15.1 %collective-permute-start.6 = (bf16[4,16,16,256]{3,2,1,0:T(8,128)(2,1)}, bf16[4,16,16,256]{3,2,1,0:T(8,128)(2,1)}, u32[]{:S(2)}, u32[]{:S(2)}) collective-permute-start(bf16[4,16,16,256]{3,2,1,0:T(8,128)(2,1)} %get-tuple-element.17.refs_1_), channel_id=1, source_target_pairs={{0,2},{1,3},{2,0},{3,1},{4,6},{5,7},{6,4},{7,5},{8,10},{9,11},{10,... | collective-permute-start | bytes 1572872 | tf_op jit(solution)/shard_map/ppermute | solution.py:16
  3.8 33.0 %collective-permute-start.5 = (bf16[4,16,16,256]{3,2,1,0:T(8,128)(2,1)}, bf16[4,16,16,256]{3,2,1,0:T(8,128)(2,1)}, u32[]{:S(2)}, u32[]{:S(2)}) collective-permute-start(bf16[4,16,16,256]{3,2,1,0:T(8,128)(2,1)} %get-tuple-element.17.refs_1_), channel_id=1, source_target_pairs={{0,1},{1,0},{2,3},{3,2},{4,5},{5,4},{6,7},{7,6},{8,9},{9,8},{10,11... | collective-permute-start | bytes 1572872 | tf_op jit(solution)/shard_map/ppermute | solution.py:16
  3.8 23.7 %collective-permute-start.1 = (bf16[4,16,16,256]{3,2,1,0:T(8,128)(2,1)}, bf16[4,16,16,256]{3,2,1,0:T(8,128)(2,1)}, u32[]{:S(2)}, u32[]{:S(2)}) collective-permute-start(bf16[4,16,16,256]{3,2,1,0:T(8,128)(2,1)} %get-tuple-element.18.refs_1_), channel_id=1, source_target_pairs={{0,2},{1,3},{2,0},{3,1},{4,6},{5,7},{6,4},{7,5},{8,10},{9,11},{10,... | collective-permute-start | bytes 1572872 | tf_op jit(solution)/shard_map/ppermute | solution.py:16
  4.3 62.4 %collective-permute-start = (bf16[4,16,16,256]{3,2,1,0:T(8,128)(2,1)}, bf16[4,16,16,256]{3,2,1,0:T(8,128)(2,1)}, u32[]{:S(2)}, u32[]{:S(2)}) collective-permute-start(bf16[4,16,16,256]{3,2,1,0:T(8,128)(2,1)} %get-tuple-element.18.refs_1_), channel_id=1, source_target_pairs={{0,1},{1,0},{2,3},{3,2},{4,5},{5,4},{6,7},{7,6},{8,9},{9,8},{10,11... | collective-permute-start | bytes 1572872 | tf_op jit(solution)/shard_map/ppermute | solution.py:16
  13.5 5.2 %copy-start.2 = (bf16[32,16,256]{2,1,0:T(8,128)(2,1)S(1)}, bf16[32,16,256]{2,1,0:T(8,128)(2,1)}, u32[]{:S(2)}) copy-start(bf16[32,16,256]{2,1,0:T(8,128)(2,1)} %param.9) | copy-start | bytes 786436
  13.5 19.2 %copy-start.6 = (bf16[4,32,256]{2,1,0:T(8,128)(2,1)S(1)}, bf16[4,32,256]{2,1,0:T(8,128)(2,1)}, u32[]{:S(2)}) copy-start(bf16[4,32,256]{2,1,0:T(8,128)(2,1)} %param.14) | copy-start | bytes 196612
  13.8 21.8 %copy-start.1 = (bf16[3,3,3,8,32]{4,3,2,1,0:T(8,128)(2,1)S(1)}, bf16[3,3,3,8,32]{4,3,2,1,0:T(8,128)(2,1)}, u32[]{:S(2)}) copy-start(bf16[3,3,3,8,32]{4,3,2,1,0:T(8,128)(2,1)} %param.16) | copy-start | bytes 41476
  17.4 15.1 %collective-permute-start.8 = (bf16[4,16,16,256]{3,2,1,0:T(8,128)(2,1)}, bf16[4,16,16,256]{3,2,1,0:T(8,128)(2,1)}, u32[]{:S(2)}, u32[]{:S(2)}) collective-permute-start(bf16[4,16,16,256]{3,2,1,0:T(8,128)(2,1)} %collective-permute-done.6.refs_3_), channel_id=1, source_target_pairs={{0,4},{1,5},{4,8},{5,9},{6,2},{7,3},{8,12},{9,13},{10,6},{11,7},{1... | collective-permute-start | bytes 1572872 | tf_op jit(solution)/shard_map/ppermute | solution.py:16
  27.5 15.6 %collective-permute-start.3 = (bf16[4,16,16,256]{3,2,1,0:T(8,128)(2,1)}, bf16[4,16,16,256]{3,2,1,0:T(8,128)(2,1)S(1)}, u32[]{:S(2)}, u32[]{:S(2)}) collective-permute-start(bf16[4,16,16,256]{3,2,1,0:T(8,128)(2,1)} %collective-permute-done.1.refs_3_), channel_id=1, source_target_pairs={{0,4},{1,5},{4,8},{5,9},{6,2},{7,3},{8,12},{9,13},{10,6},{11,7},{1... | collective-permute-start | bytes 1572872 | tf_op jit(solution)/shard_map/ppermute | solution.py:16
  28.8 14.3 %collective-permute-start.7 = (bf16[4,16,16,256]{3,2,1,0:T(8,128)(2,1)}, bf16[4,16,16,256]{3,2,1,0:T(8,128)(2,1)}, u32[]{:S(2)}, u32[]{:S(2)}) collective-permute-start(bf16[4,16,16,256]{3,2,1,0:T(8,128)(2,1)} %collective-permute-done.6.refs_3_), channel_id=1, source_target_pairs={{0,1},{1,0},{2,3},{3,2},{4,5},{5,4},{6,7},{7,6},{8,9},{9,8},{10,11... | collective-permute-start | bytes 1572872 | tf_op jit(solution)/shard_map/ppermute | solution.py:16
  32.5 10.5 %collective-permute-start.9 = (bf16[4,16,16,256]{3,2,1,0:T(8,128)(2,1)}, bf16[4,16,16,256]{3,2,1,0:T(8,128)(2,1)}, u32[]{:S(2)}, u32[]{:S(2)}) collective-permute-start(bf16[4,16,16,256]{3,2,1,0:T(8,128)(2,1)} %collective-permute-done.8.refs_5_), channel_id=1, source_target_pairs={{0,1},{1,0},{2,3},{3,2},{4,5},{5,4},{6,7},{7,6},{8,9},{9,8},{10,11... | collective-permute-start | bytes 1572872 | tf_op jit(solution)/shard_map/ppermute | solution.py:16
  36.8 29.8 %collective-permute-start.2 = (bf16[4,16,16,256]{3,2,1,0:T(8,128)(2,1)}, bf16[4,16,16,256]{3,2,1,0:T(8,128)(2,1)S(1)}, u32[]{:S(2)}, u32[]{:S(2)}) collective-permute-start(bf16[4,16,16,256]{3,2,1,0:T(8,128)(2,1)} %collective-permute-done.1.refs_3_), channel_id=1, source_target_pairs={{0,1},{1,0},{2,3},{3,2},{4,5},{5,4},{6,7},{7,6},{8,9},{9,8},{10,11... | collective-permute-start | bytes 1572872 | tf_op jit(solution)/shard_map/ppermute | solution.py:16
  43.0 23.6 %copy-start.8 = (bf16[4,16,16,256]{3,2,1,0:T(8,128)(2,1)}, bf16[4,16,16,256]{3,2,1,0:T(8,128)(2,1)S(1)}, u32[]{:S(2)}) copy-start(bf16[4,16,16,256]{3,2,1,0:T(8,128)(2,1)S(1)} %collective-permute-done.3.refs_5_) | copy-start | bytes 1572868
  43.0 23.6 %collective-permute-start.4 = (bf16[4,16,16,256]{3,2,1,0:T(8,128)(2,1)S(1)}, bf16[4,16,16,256]{3,2,1,0:T(8,128)(2,1)S(1)}, u32[]{:S(2)}, u32[]{:S(2)}) collective-permute-start(bf16[4,16,16,256]{3,2,1,0:T(8,128)(2,1)S(1)} %collective-permute-done.3.refs_5_), channel_id=1, source_target_pairs={{0,1},{1,0},{2,3},{3,2},{4,5},{5,4},{6,7},{7,6},{8,9},{9,8},{10,11... | collective-permute-start | bytes 1572872 | tf_op jit(solution)/shard_map/ppermute | solution.py:16
  66.7 0.8 copy-start.9
  66.7 1.0 copy-start.10
  93.7 35.3 %collective-permute-start.10 = (bf16[256,256]{1,0:T(8,128)(2,1)}, bf16[256,256]{1,0:T(8,128)(2,1)S(1)}, u32[]{:S(2)}, u32[]{:S(2)}) collective-permute-start(bf16[256,256]{1,0:T(8,128)(2,1)} %get-tuple-element.15), channel_id=1, source_target_pairs={{0,1},{1,2},{2,3},{3,4},{4,5},{5,6},{6,7},{7,8},{8,9},{9,10},{10,1... | collective-permute-start | bytes 393224 | tf_op jit(solution)/shard_map/ppermute | solution.py:16
  96.0 33.1 %collective-permute-start.11 = (bf16[256,256]{1,0:T(8,128)(2,1)}, bf16[256,256]{1,0:T(8,128)(2,1)S(1)}, u32[]{:S(2)}, u32[]{:S(2)}) collective-permute-start(bf16[256,256]{1,0:T(8,128)(2,1)} %get-tuple-element.16), channel_id=1, source_target_pairs={{1,0},{2,1},{3,2},{4,3},{5,4},{6,5},{7,6},{8,7},{9,8},{10,9},{11,1... | collective-permute-start | bytes 393224 | tf_op jit(solution)/shard_map/ppermute | solution.py:16
  107.3 8.2 %copy-start = (bf16[3,9,8,3,32,8]{4,1,2,0,3,5:T(8,128)(2,1)S(1)}, bf16[3,9,8,3,32,8]{4,1,2,0,3,5:T(8,128)(2,1)}, u32[]{:S(2)}) copy-start(bf16[3,9,8,3,32,8]{4,1,2,0,3,5:T(8,128)(2,1)} %convolution_bitcast_fusion.1) | copy-start | bytes 995332
  129.1 0.7 copy-start.3
  129.1 0.7 copy-start.4

commit v2 on v1

v2 whole, which is shorter than its diff:
```python
import jax
import jax.numpy as jnp
from jax import lax
from jax.experimental import pallas as pl
from jax.experimental.pallas import tpu as pltpu
from jax.sharding import PartitionSpec as P

MIB = 1024 * 1024
CHUNKS = (16, 16)
LANES = 128
WIDE = 8
UNROLL = 4
GROUP = 8


def routed(x, target):
    length = lax.axis_size("tile")
    pairs = [(i, target(i)) for i in range(length) if 0 <= target(i) < length]
    return lax.ppermute(x, "tile", pairs)


def onward(i):
    return i + 4 if i % 4 < 2 else i - 4


def strip_offsets(tile):
    low = (tile % 4) < 2
    across = jnp.where(low, 2, -2)
    along = -across
    beside = jnp.where(tile % 2 == 0, 1, -1)
    return jnp.stack([tile, tile + beside, tile + across, tile + beside + across, tile + along, tile + beside + along])


def column_kernel(views, cols, tap_ref, frac_ref, out_ref):
    index = lax.broadcasted_iota(jnp.int32, (cols, cols), 0).astype(jnp.bfloat16)
    zero = jnp.zeros((), jnp.bfloat16)

    def plane(d, _):
        for v in range(views):
            tap = tap_ref[v, pl.ds(d, 1), :]
            frac = frac_ref[v, pl.ds(d, 1), :]
            upper = jnp.where(index == (tap + 1.0).astype(jnp.bfloat16), frac.astype(jnp.bfloat16), zero)
            out_ref[d, v] = jnp.where(index == tap.astype(jnp.bfloat16), (1.0 - frac).astype(jnp.bfloat16), upper)
        return 0

    lax.fori_loop(0, tap_ref.shape[1], plane, 0)


def column_matrices(tap, frac):
    views, planes, cols = tap.shape
    vmem = pl.BlockSpec(memory_space=pltpu.VMEM)

    def kernel(*refs):
        column_kernel(views, cols, *refs)

    return pl.pallas_call(
        kernel,
        out_shape=jax.ShapeDtypeStruct((planes, views, cols, cols), jnp.bfloat16),
        in_specs=[vmem, vmem],
        out_specs=vmem,
        compiler_params=pltpu.CompilerParams(vmem_limit_bytes=20 * MIB),
        name="columns",
    )(tap, frac)


def warp_kernel(strips, views, planes, chans, rows, cols, *refs):
    inv_ref, refs = refs[0], refs[1:]
    strip_refs, refs = refs[:strips], refs[strips:]
    base_ref, rowmat_ref, colmat_ref, var_ref, edge_ref, rowmix, even, odd = refs
    count = chans * rows
    half = rows // 2
    depth = rowmat_ref.shape[2]
    wide = max(w for w in range(1, WIDE + 1) if chans % w == 0)
    blank = jnp.zeros((depth - strips * rows, cols), jnp.bfloat16)

    def mix_rows(c, _):
        for v in range(views):
            bands = [
                jnp.concatenate([s[v, c * wide + k] for s in strip_refs] + [blank], axis=0) for k in range(wide)
            ]
            band = jnp.concatenate(bands, axis=1)
            for start in range(0, planes, 8):
                lhs = rowmat_ref[v, start * rows : (start + 8) * rows, :]
                mixed = jnp.dot(lhs, band, preferred_element_type=jnp.float32).astype(jnp.bfloat16)
                for k in range(wide):
                    at = pl.ds(pl.multiple_of((c * wide + k) * rows, rows), rows)
                    rowmix[v, start : start + 8, at, :] = mixed[:, k * cols : (k + 1) * cols].reshape(8, rows, cols)
        return 0

    lax.fori_loop(0, chans // wide, mix_rows, 0)
    inv = inv_ref[0, 0]

    def warp_plane(d, warped):
        for v in range(views):
            warped[v] = jnp.dot(rowmix[v, d], colmat_ref[d, v], preferred_element_type=jnp.float32)

    def finish_plane(d, warped):
        for c in range(0, chans, 2):
            total = base_ref[c : c + 2].reshape(2 * rows, cols)
            squares = total * total
            for v in range(views):
                term = warped[v, c * rows : (c + 2) * rows, :]
                total = total + term
                squares = squares + term * term
            var = (squares - total * (total * inv)).reshape(2, 2, half, cols)
            for h in range(2):
                var_ref[d, h, c * half : (c + 2) * half, :] = var[:, h].reshape(2 * half, cols).astype(jnp.bfloat16)
                edge_ref[h, d, c : c + 2, :] = var[:, h, h * (half - 1)]

    slots = (even, odd)
    warp_plane(0, even)

    def step(i, _):
        for k in range(UNROLL):
            d = i * UNROLL + k
            warp_plane(jnp.minimum(d + 1, planes - 1), slots[(k + 1) % 2])
            finish_plane(d, slots[k % 2])
        return 0

    lax.fori_loop(0, planes // UNROLL, step, 0)


def warp(inv, strips, base, rowmat, colmat):
    views, size, rows, cols = strips[0].shape
    planes = colmat.shape[0]
    vmem = pl.BlockSpec(memory_space=pltpu.VMEM)

    def kernel(*refs):
        warp_kernel(len(strips), views, planes, size, rows, cols, *refs)

    return pl.pallas_call(
        kernel,
        out_shape=(
            jax.ShapeDtypeStruct((planes, 2, size * rows // 2, cols), jnp.bfloat16),
            jax.ShapeDtypeStruct((2, planes, size, cols), jnp.float32),
        ),
        in_specs=[pl.BlockSpec(memory_space=pltpu.SMEM)] + [vmem] * (len(strips) + 3),
        out_specs=(vmem, vmem),
        scratch_shapes=[
            pltpu.VMEM((views, planes, size * rows, cols), jnp.bfloat16),
            pltpu.VMEM((views, size * rows, cols), jnp.float32),
            pltpu.VMEM((views, size * rows, cols), jnp.float32),
        ],
        compiler_params=pltpu.CompilerParams(vmem_limit_bytes=22 * MIB),
        cost_estimate=pl.CostEstimate(
            flops=2 * views * planes * size * rows * cols * cols * 2, bytes_accessed=4 << 20, transcendentals=0
        ),
        name="warp",
    )(inv, *strips, base, rowmat, colmat)


def joined_columns(terms, outs):
    cols = terms.shape[-1]
    terms = terms.reshape(-1, 3, outs, cols)
    left, middle, right = [terms[:, e].reshape(-1, cols) for e in range(3)]
    lane = lax.broadcasted_iota(jnp.int32, middle.shape, 1)
    left = jnp.where(lane == 0, 0.0, pltpu.roll(left, 1, 1))
    right = jnp.where(lane == cols - 1, 0.0, pltpu.roll(right, cols - 1, 1))
    return middle + left + right


def edge_kernel(planes, group, outs, cols, nchunks, inv_ref, *refs):
    edge_refs, (mat_ref, up_ref, down_ref, acc) = refs[:nchunks], refs[nchunks:]
    for side, out in ((0, up_ref), (1, down_ref)):
        acc[...] = jnp.zeros_like(acc)
        for start in range(0, planes, group):
            rhs = jnp.concatenate([e[side, start : start + group].reshape(-1, cols) for e in edge_refs], axis=0)
            terms = jnp.dot(mat_ref[side], rhs.astype(jnp.bfloat16), preferred_element_type=jnp.float32)
            rows = (group + 2) * outs
            acc[start * outs : start * outs + rows] += joined_columns(terms, outs)
        out[...] = (acc[outs : outs + planes * outs] * inv_ref[0, 0]).astype(jnp.bfloat16)


def edge_terms(inv, edges, mat, outs):
    planes, cols = edges[0].shape[1], edges[0].shape[3]
    group = mat.shape[1] // (3 * outs) - 2
    vmem = pl.BlockSpec(memory_space=pltpu.VMEM)

    def kernel(*refs):
        edge_kernel(planes, group, outs, cols, len(edges), *refs)

    shape = jax.ShapeDtypeStruct((planes * outs, cols), jnp.bfloat16)
    return pl.pallas_call(
        kernel,
        out_shape=(shape, shape),
        in_specs=[pl.BlockSpec(memory_space=pltpu.SMEM)] + [vmem] * (len(edges) + 1),
        out_specs=(vmem, vmem),
        scratch_shapes=[pltpu.VMEM(((planes + 2) * outs, cols), jnp.float32)],
        compiler_params=pltpu.CompilerParams(vmem_limit_bytes=16 * MIB),
        name="edge",
    )(inv, *edges, mat)


def filter_kernel(planes, start, count, rows, outs, cols, nchunks, *refs):
    inv_ref, bias_ref, refs = refs[0], refs[1], refs[2:]
    var_refs, refs = refs[:nchunks], refs[nchunks:]
    first = start == 0
    if first:
        mat_ref, out_ref = refs
    else:
        mat_ref, early_ref, above_ref, below_ref, out_ref, *flats = refs
    half = rows // 2
    inv = inv_ref[0, 0]

    def block(d, h, exists):
        found = jnp.concatenate([v[d, h] for v in var_refs], axis=0)
        return found if exists is None else found * exists.astype(jnp.float32).astype(jnp.bfloat16)

    def sums(d, k):
        parts = []
        for h in range(2):
            before = block(jnp.maximum(d - 1, 0), h, d > 0 if first and k == 0 else None)
            after = block(jnp.minimum(d + 1, planes - 1), h, d < planes - 1 if not first and k == UNROLL - 1 else None)
            rhs = jnp.concatenate([before, block(d, h, None), after], axis=0)
            terms = jnp.dot(mat_ref[h], rhs, preferred_element_type=jnp.float32)
            parts.append(joined_columns(terms, outs) * inv)
        upper, lower = parts
        return jnp.concatenate(
            [upper[: (half - 1) * outs], upper[(half - 1) * outs :] + lower[: 2 * outs], lower[2 * outs :]]
        )

    def finish(d, whole, flat):
        at = pl.multiple_of(d * outs, outs)
        whole = jnp.concatenate(
            [
                whole[:outs] + above_ref[pl.ds(at, outs), :].astype(jnp.float32),
                whole[outs:-outs],
                whole[-outs:] + below_ref[pl.ds(at, outs), :].astype(jnp.float32),
            ]
        )
        for lane in range(cols // LANES):
            lanes = slice(lane * LANES, (lane + 1) * LANES)
            flat[lane] = whole[:, lanes]
            for o in range(outs):
                out_ref[d, o, :, lanes] = (flat[lane, pl.ds(o, rows, stride=outs), :] + bias_ref[0, o]).astype(jnp.bfloat16)

    def step(i, _):
        for k in range(UNROLL):
            at = i * UNROLL + k
            whole = sums(start + at, k)
            if first:
                out_ref[at] = whole
            else:
                finish(at, early_ref[at], flats[2 * k])
                finish(start + at, whole, flats[2 * k + 1])
        return 0

    lax.fori_loop(0, count // UNROLL, step, 0)


def filtered(inv, bias, variances, mat, rows, outs, early=None, above=None, below=None):
    planes, _, _, cols = variances[0].shape
    vmem = pl.BlockSpec(memory_space=pltpu.VMEM)
    smem = pl.BlockSpec(memory_space=pltpu.SMEM)
    count = planes // 2
    first = early is None
    more = [] if first else [early, above, below]

    def kernel(*refs):
        filter_kernel(planes, 0 if first else count, count, rows, outs, cols, len(variances), *refs)

    return pl.pallas_call(
        kernel,
        out_shape=jax.ShapeDtypeStruct((count, rows * outs, cols), jnp.float32)
        if first
        else jax.ShapeDtypeStruct((planes, outs, rows, cols), jnp.bfloat16),
        in_specs=[smem, smem] + [vmem] * (len(variances) + 1 + len(more)),
        out_specs=vmem,
        scratch_shapes=[]
        if first
        else [pltpu.VMEM((cols // LANES, rows * outs, LANES), jnp.float32)] * (2 * UNROLL),
        compiler_params=pltpu.CompilerParams(vmem_limit_bytes=20 * MIB),
        cost_estimate=pl.CostEstimate(
            flops=2 * count * 2 * mat.shape[1] * mat.shape[2] * cols, bytes_accessed=8 << 20, transcendentals=0
        ),
        name="filter",
    )(inv, bias, *variances, mat, *more)


def matrix_kernel(chunks, group, weight_ref, filter_ref, edge_ref):
    taps, each, chans = weight_ref.shape
    half = filter_ref.shape[1] // each - 1
    width = chans * half
    weight = weight_ref[...].reshape(taps * each, chans)
    chan = lax.broadcasted_iota(jnp.int32, (chans, width), 0)
    lane = lax.broadcasted_iota(jnp.int32, (chans, width), 1)

    def spread(mask):
        onehot = jnp.where(mask, 1.0, 0.0).astype(jnp.bfloat16)
        return jnp.dot(weight, onehot, preferred_element_type=jnp.float32).reshape(taps, each, width)

    by_row = [spread(lane == chan * half + r) for r in range(half)]
    for h in range(2):
        for a in range(3):
            rows = []
            for g in range(half + 1):
                row = jnp.zeros((each, width), jnp.float32)
                for b in range(3):
                    r = g - h + b - 1
                    if 0 <= r < half:
                        row = row + by_row[r][3 * a + b]
                rows.append(row)
            filter_ref[h, :, a * width : (a + 1) * width] = jnp.concatenate(rows).astype(jnp.bfloat16)
    by_plane = []
    for q in range(group):
        mask = chan < 0
        offset = 0
        for size in chunks:
            here = (chan >= offset) & (chan < offset + size)
            mask = mask | (here & (lane == chan + offset * (group - 1) + q * size))
            offset += size
        by_plane.append(spread(mask))
    for side, b in ((0, 2), (1, 0)):
        rows = []
        for p in range(group + 2):
            row = jnp.zeros((each, width), jnp.float32)
            for a in range(3):
                q = a + p - 2
                if 0 <= q < group:
                    row = row + by_plane[q][3 * a + b]
            rows.append(row)
        edge_ref[side] = jnp.concatenate(rows).astype(jnp.bfloat16)


def matrices(weight, rows, chunks, group):
    outs, chans = weight.shape[3:]
    each = 3 * outs
    half = rows // 2
    vmem = pl.BlockSpec(memory_space=pltpu.VMEM)

    def kernel(*refs):
        matrix_kernel(chunks, group, *refs)

    return pl.pallas_call(
        kernel,
        out_shape=(
            jax.ShapeDtypeStruct((2, (half + 1) * each, 3 * chans * half), jnp.bfloat16),
            jax.ShapeDtypeStruct((2, (group + 2) * each, group * chans), jnp.bfloat16),
        ),
        in_specs=[vmem],
        out_specs=(vmem, vmem),
        compiler_params=pltpu.CompilerParams(vmem_limit_bytes=16 * MIB),
        name="matrices",
    )(weight.reshape(9, each, chans))


def on_device(
    ref_feat, src_feat, row_tap, row_frac, col_tap, col_frac, view_count, conv_weight, conv_bias
):
    rows = ref_feat.shape[1]
    views = src_feat.shape[0]
    planes = row_tap.shape[1]
    outs = conv_weight.shape[3]
    tile = lax.axis_index("tile")

    starts = strip_offsets(tile) * rows
    index = (starts[:, None] + jnp.arange(rows)).reshape(-1)
    index = jnp.pad(index, (0, LANES - index.shape[0]), constant_values=-2)
    keep = (1.0 - row_frac.astype(jnp.float32)).astype(jnp.bfloat16)
    valid = (jnp.arange(views) < view_count[0])[:, None, None, None]
    zero = jnp.zeros((), jnp.bfloat16)
    rowmat = jnp.where(
        (index == row_tap[..., None]) & valid,
        keep[..., None],
        jnp.where((index == row_tap[..., None] + 1) & valid, row_frac[..., None], zero),
    ).reshape(views, planes * rows, -1)
    inv = (1.0 / (1.0 + view_count.astype(jnp.float32))).reshape(1, 1)
    frac = col_frac.astype(jnp.float32)
    colmat = column_matrices(col_tap.astype(jnp.float32), frac)
    base = ref_feat.astype(jnp.float32)
    filter_mat, edge_mat = matrices(conv_weight, rows, CHUNKS, GROUP)

    spans = [slice(sum(CHUNKS[:i]), sum(CHUNKS[: i + 1])) for i in range(len(CHUNKS))]
    pieces = [src_feat[:, span] for span in spans]
    pieces[1:] = lax.optimization_barrier(pieces[1:])
    across = [routed(piece, lambda i: i ^ 2) for piece in pieces]
    beside = [routed(piece, lambda i: i ^ 1) for piece in pieces]
    bases = [base[span] for span in spans]
    across[0], rowmat, colmat, bases, filter_mat, edge_mat = lax.optimization_barrier(
        (across[0], rowmat, colmat, bases, filter_mat, edge_mat)
    )
    variances = []
    edges = []
    along = routed(across[0], onward)
    across_beside = routed(across[0], lambda i: i ^ 1)
    for i in range(len(CHUNKS)):
        along_beside = routed(along, lambda i: i ^ 1)
        strips = [pieces[i], beside[i], across[i], across_beside, along, along_beside]
        if i + 1 < len(CHUNKS):
            along = routed(across[i + 1], onward)
            across_beside = routed(across[i + 1], lambda i: i ^ 1)
        var, edge = warp(inv, strips, bases[i], rowmat, colmat)
        if i + 1 < len(CHUNKS):
            var, edge, along, across_beside, across[i + 2 :] = lax.optimization_barrier(
                (var, edge, along, across_beside, across[i + 2 :])
            )
        variances.append(var)
        edges.append(edge)
    up, down = edge_terms(inv, edges, edge_mat, outs)
    above = routed(down, lambda i: i + 1)
    below = routed(up, lambda i: i - 1)
    bias = conv_bias.reshape(1, -1)
    early = filtered(inv, bias, variances, filter_mat, rows, outs)
    return filtered(inv, bias, variances, filter_mat, rows, outs, early, above, below)


def solution(mesh):
    placed = (
        P("groups", "tile", None),
        P("groups", None, "tile", None),
        P("groups", None, "tile"),
        P("groups", None, "tile"),
        P("groups", None, None),
        P("groups", None, None),
        P(("groups", "tile")),
        P(),
        P(),
    )
    return jax.shard_map(
        on_device,
        mesh=mesh,
        in_specs=placed,
        out_specs=P("groups", None, "tile", None),
        check_vma=False,
    )
```

time: 150 us -> 81.4 us (0.54)
  local copies, waits for them, and re-layouts: 36.4 us -> 4.55 us
  Pallas kernels: 69.2 us -> 40.2 us
  matrix products: 5.2 us -> 0 us
  waiting for transfers between devices: 19.2 us -> 15.8 us
  starting transfers between devices: 12.1 us -> 13.8 us
    pallas_call x4 -> x7, Pallas kernels: 69.2 us -> 40.2 us  [the longest x2 24.8 us: warp(): pl.pallas_call(kernel, out_shape=(jax.ShapeDtypeStruct((planes, 2, size *...]
    another operation x2 -> x0, local copies, waits for them, and re-layouts: 16.2 us -> none  [filter_matrix(): return jnp.stack(mats)]
    transpose x6 -> x0, local copies, waits for them, and re-layouts: 11.4 us -> none  [the longest x2 9.32 us: filter_matrix(): jnp.einsum('grb,abeoc->egoacr', pick, weight)]
    dot_general x6 -> x0, matrix products: 5.2 us -> none  [the longest x2 3.37 us: filter_matrix(): jnp.einsum('grb,abeoc->egoacr', pick, weight)]
    ppermute x12, waiting for transfers between devices: 19.2 us -> 15.8 us  [routed(): return lax.ppermute(x, 'tile', pairs)]
    slice x3 -> x2, local copies, waits for them, and re-layouts: 3.85 us -> 1.35 us  [the longest x1 1.3 us: on_device(): pieces = [src_feat[:, span] for span in spans]]
    reshape x4 -> x0, local copies, waits for them, and re-layouts: 2.34 us -> none  [edge_matrix(): jnp.einsum('pqa,aeoc->epoqc', pick, part)]
    ppermute x12, starting transfers between devices: 12.1 us -> 13.8 us  [routed(): return lax.ppermute(x, 'tile', pairs)]
  transfers between devices with their start and end apart: 12 -> 12, of which waited for: 4 -> 3; matrix products, arithmetic and copies ran while one was open for 29% -> 9% of each run, Pallas kernels for 16% -> 26%
where the time goes in v2:
time: 81.4 us; the launch traced here: 80.1 us
  Pallas kernels  40.2 us (49%)
  waiting for transfers between devices  15.8 us (19%)
  starting transfers between devices  13.8 us (17%)
  other arithmetic  4.77 us (6%)
  local copies, waits for them, and re-layouts  4.55 us (6%)
  between operations  0.94 us (1%)
    pallas_call x2, Pallas kernels, warp(): pl.pallas_call(kernel, out_shape=(jax.ShapeDtypeStruct((planes, 2, size *...  24.8 us
    ppermute x12, waiting for transfers between devices, routed(): return lax.ppermute(x, 'tile', pairs)  15.8 us
    ppermute x12, starting transfers between devices, routed(): return lax.ppermute(x, 'tile', pairs)  13.8 us
    pallas_call x2, Pallas kernels, filtered(): pl.pallas_call(kernel, out_shape=jax.ShapeDtypeStruct((count, rows * outs...  10.8 us
    pallas_call x1, Pallas kernels, column_matrices(): pl.pallas_call(kernel, out_shape=jax.ShapeDtypeStruct((planes, views, col...  3.4 us
    unnamed x8, local copies, waits for them, and re-layouts  2.46 us
  transfers between devices with their start and end apart: 12, of which 3 were waited for; matrix products, arithmetic and copies ran while one was open for 9% of the time, Pallas kernels for 26%

profile of v2, /device:TPU:24, one launch (start us, length us, event | category | flops | bytes accessed | tf_op | source)
XLA Modules:
  0.0 80.1 jit_solution(3540989994055505937)
XLA Ops:
  0.0 1.3 %fusion = (bf16[4,16,16,256]{3,2,1,0:T(8,128)(2,1)S(1)}, bf16[4,16,16,256]{3,2,1,0:T(8,128)(2,1)S(1)}) fusion(bf16[4,32,16,256]{3,2,1,0:T(8,128)(2,1)} %param.10), kind=kLoop, calls=%fused_computation.7 | loop fusion | bytes 2097152 | tf_op jit(solution)/shard_map/slice | solution.py:374
  1.3 1.6 %collective-permute-start.1 = (bf16[4,16,16,256]{3,2,1,0:T(8,128)(2,1)S(1)}, bf16[4,16,16,256]{3,2,1,0:T(8,128)(2,1)S(1)}, u32[]{:S(2)}, u32[]{:S(2)}) collective-permute-start(bf16[4,16,16,256]{3,2,1,0:T(8,128)(2,1)S(1)} %get-tuple-element.44.refs_1_), channel_id=1, source_target_pairs={{0,2},{1,3},{2,0},{3,1},{4,6},{5,7},{6,4},{7,5},{8,10},{9,11},{10,... | collective-permute-start | bytes 1572872 | tf_op jit(solution)/shard_map/ppermute | solution.py:19
  3.7 0.7 subtract_convert_fusion
  4.4 0.8 broadcast_add_fusion
  5.2 0.8 %copy.13 = bf16[4,32,16]{2,1,0:T(8,128)(2,1)S(1)} copy(bf16[4,32,16]{1,2,0:T(8,128)(2,1)} %param.12) | data formatting | bytes 8192 | tf_op args[3]
  6.0 0.8 %copy.10 = s32[4,32,16]{2,1,0:T(8,128)S(1)} copy(s32[4,32,16]{1,2,0:T(8,128)} %param.11) | data formatting | bytes 16384 | tf_op args[2]
  6.9 0.1 copy.11
  7.0 0.1 broadcast_in_dim.33
  7.2 0.1 eq.41
  7.3 0.1 broadcast_in_dim.35
  7.4 0.1 eq.38
  7.5 0.9 %convert_element_type.21.refs_0_ = f32[4,32,256]{2,1,0:T(8,128)S(1)} convert(s32[4,32,256]{2,1,0:T(8,128)} %param.13) | non-fusion elementwise | flops 32768 | bytes 262144 | tf_op jit(solution)/shard_map/convert_element_type | solution.py:369
  8.4 0.9 %convert_element_type.22.refs_1_ = f32[4,32,256]{2,1,0:T(8,128)S(1)} convert(bf16[4,32,256]{2,1,0:T(8,128)(2,1)} %param.14) | non-fusion elementwise | flops 32768 | bytes 196608 | tf_op jit(solution)/shard_map/convert_element_type | solution.py:368
  9.3 0.8 %copy-done = bf16[3,3,3,8,32]{4,3,2,1,0:T(8,128)(2,1)S(1)} copy-done((bf16[3,3,3,8,32]{4,3,2,1,0:T(8,128)(2,1)S(1)}, bf16[3,3,3,8,32]{4,3,2,1,0:T(8,128)(2,1)}, u32[]{:S(2)}) %copy-start) | copy-done | bytes 13848
  10.1 0.6 matrices.1
  10.8 3.4 %columns.1.refs_9_ = bf16[32,4,256,256]{3,2,1,0:T(8,128)(2,1)S(1)} custom-call(f32[4,32,256]{2,1,0:T(8,128)S(1)} %convert_element_type.21.refs_0_, f32[4,32,256]{2,1,0:T(8,128)S(1)} %convert_element_type.22.refs_1_), custom_call_target="tpu_custom_call" | custom-call | tf_op jit(solution)/shard_map/columns/pallas_call | solution.py:56
  14.2 1.4 %and_select_fusion.1.refs_8_ = bf16[4,512,128]{2,1,0:T(8,128)(2,1)S(1)} fusion(s32[4,512]{1,0:T(4,128)S(1)} %eq.41, s32[4,512]{1,0:T(4,128)S(1)} %eq.38, s32[128]{0:T(128)S(1)} %pad.4, pred[4]{0:T(512)(128)(4,1)S(1)} %iota_compare_fusion, bf16[4,512]{1,0:T(4,128)(2,1)S(1)} %broadcast_in_dim.35, bf16[4,512]{1,0:T(4,128)(2,1)S(1)} %broadcast_in_dim.33), kind=kLoop, calls=%fused_computation.1 | loop fusion | flops 1572864 | bytes 549380 | tf_op jit(solution)/shard_map/jit(_where)/select_n | solution.py:362
  15.7 1.3 %collective-permute-start.3 = (bf16[4,16,16,256]{3,2,1,0:T(8,128)(2,1)S(1)}, bf16[4,16,16,256]{3,2,1,0:T(8,128)(2,1)S(1)}, u32[]{:S(2)}, u32[]{:S(2)}) collective-permute-start(bf16[4,16,16,256]{3,2,1,0:T(8,128)(2,1)S(1)} %collective-permute-done.1.refs_3_), channel_id=1, source_target_pairs={{0,4},{1,5},{4,8},{5,9},{6,2},{7,3},{8,12},{9,13},{10,6},{11,7},{1... | collective-permute-start | bytes 1572872 | tf_op jit(solution)/shard_map/ppermute | solution.py:19
  17.0 2.0 %collective-permute-start.5 = (bf16[4,16,16,256]{3,2,1,0:T(8,128)(2,1)S(1)}, bf16[4,16,16,256]{3,2,1,0:T(8,128)(2,1)S(1)}, u32[]{:S(2)}, u32[]{:S(2)}) collective-permute-start(bf16[4,16,16,256]{3,2,1,0:T(8,128)(2,1)S(1)} %get-tuple-element.43.refs_1_), channel_id=1, source_target_pairs={{0,2},{1,3},{2,0},{3,1},{4,6},{5,7},{6,4},{7,5},{8,10},{9,11},{10,... | collective-permute-start | bytes 1572872 | tf_op jit(solution)/shard_map/ppermute | solution.py:19
  19.0 0.5 collective-permute-start.2
  19.5 11.4 %collective-permute-done.3.refs_5_ = bf16[4,16,16,256]{3,2,1,0:T(8,128)(2,1)S(1)} collective-permute-done((bf16[4,16,16,256]{3,2,1,0:T(8,128)(2,1)S(1)}, bf16[4,16,16,256]{3,2,1,0:T(8,128)(2,1)S(1)}, u32[]{:S(2)}, u32[]{:S(2)}) %collective-permute-start.3) | collective-permute-done | bytes 524320 | tf_op jit(solution)/shard_map/ppermute | solution.py:19
  30.9 0.5 collective-permute-start.8
  31.6 1.3 %collective-permute-start.6 = (bf16[4,16,16,256]{3,2,1,0:T(8,128)(2,1)S(1)}, bf16[4,16,16,256]{3,2,1,0:T(8,128)(2,1)S(1)}, u32[]{:S(2)}, u32[]{:S(2)}) collective-permute-start(bf16[4,16,16,256]{3,2,1,0:T(8,128)(2,1)S(1)} %collective-permute-done.5.refs_3_), channel_id=1, source_target_pairs={{0,4},{1,5},{4,8},{5,9},{6,2},{7,3},{8,12},{9,13},{10,6},{11,7},{1... | collective-permute-start | bytes 1572872 | tf_op jit(solution)/shard_map/ppermute | solution.py:19
  32.9 12.4 %warp.2 = (bf16[32,2,128,256]{3,2,1,0:T(8,128)(2,1)S(1)}, f32[2,32,16,256]{3,2,1,0:T(8,128)S(1)}) custom-call(f32[1,1]{1,0:T(1,128)} %bitcast.refs_0_, bf16[4,16,16,256]{3,2,1,0:T(8,128)(2,1)S(1)} %get-tuple-element.44.refs_1_, bf16[4,16,16,256]{3,2,1,0:T(8,128)(2,1)S(1)} %collective-permute-done.refs_2_, ...), custom_call_target="tpu_custom_call" | custom-call | flops 8589934592 | bytes 4194304 | tf_op jit(solution)/shard_map/warp/pallas_call | solution.py:131
  45.4 2.4 %collective-permute-done.6.refs_5_ = bf16[4,16,16,256]{3,2,1,0:T(8,128)(2,1)S(1)} collective-permute-done((bf16[4,16,16,256]{3,2,1,0:T(8,128)(2,1)S(1)}, bf16[4,16,16,256]{3,2,1,0:T(8,128)(2,1)S(1)}, u32[]{:S(2)}, u32[]{:S(2)}) %collective-permute-start.6) | collective-permute-done | bytes 524320 | tf_op jit(solution)/shard_map/ppermute | solution.py:19
  47.8 1.9 %collective-permute-done.9.refs_6_ = bf16[4,16,16,256]{3,2,1,0:T(8,128)(2,1)S(1)} collective-permute-done((bf16[4,16,16,256]{3,2,1,0:T(8,128)(2,1)S(1)}, bf16[4,16,16,256]{3,2,1,0:T(8,128)(2,1)S(1)}, u32[]{:S(2)}, u32[]{:S(2)}) %collective-permute-start.9) | collective-permute-done | bytes 524320 | tf_op jit(solution)/shard_map/ppermute | solution.py:19
  49.7 12.4 %warp.3 = (bf16[32,2,128,256]{3,2,1,0:T(8,128)(2,1)S(1)}, f32[2,32,16,256]{3,2,1,0:T(8,128)S(1)}) custom-call(f32[1,1]{1,0:T(1,128)} %bitcast.refs_0_, bf16[4,16,16,256]{3,2,1,0:T(8,128)(2,1)S(1)} %get-tuple-element.43.refs_1_, bf16[4,16,16,256]{3,2,1,0:T(8,128)(2,1)S(1)} %collective-permute-done.8.refs_2_, ...), custom_call_target="tpu_custom_call" | custom-call | flops 8589934592 | bytes 4194304 | tf_op jit(solution)/shard_map/warp/pallas_call | solution.py:131
  62.1 0.6 edge.1
  62.7 2.0 %collective-permute-start.10 = (bf16[256,256]{1,0:T(8,128)(2,1)S(1)}, bf16[256,256]{1,0:T(8,128)(2,1)S(1)}, u32[]{:S(2)}, u32[]{:S(2)}) collective-permute-start(bf16[256,256]{1,0:T(8,128)(2,1)S(1)} %get-tuple-element.41), channel_id=1, source_target_pairs={{0,1},{1,2},{2,3},{3,4},{4,5},{5,6},{6,7},{7,8},{8,9},{9,10},{10,1... | collective-permute-start | bytes 393224 | tf_op jit(solution)/shard_map/ppermute | solution.py:19
  64.7 4.4 %collective-permute-start.11 = (bf16[256,256]{1,0:T(8,128)(2,1)S(1)}, bf16[256,256]{1,0:T(8,128)(2,1)S(1)}, u32[]{:S(2)}, u32[]{:S(2)}) collective-permute-start(bf16[256,256]{1,0:T(8,128)(2,1)S(1)} %get-tuple-element.42), channel_id=1, source_target_pairs={{1,0},{2,1},{3,2},{4,3},{5,4},{6,5},{7,6},{8,7},{9,8},{10,9},{11,1... | collective-permute-start | bytes 393224 | tf_op jit(solution)/shard_map/ppermute | solution.py:19
  69.2 4.5 %filter.2.refs_5_ = f32[16,128,256]{2,1,0:T(8,128)S(1)} custom-call(f32[1,1]{1,0:T(1,128)} %bitcast.refs_0_, f32[1,8]{1,0:T(1,128)S(1)} %bitcast.12, bf16[32,2,128,256]{3,2,1,0:T(8,128)(2,1)S(1)} %get-tuple-element.32.refs_2_, bf16[32,2,128,256]{3,2,1,0:T(8,128)(2,1)S(1)} %get-tuple-element.36.refs_3_, bf16[2,216,768]{2,1,0:T(8,128)(2,1)S(1)} %get-tuple-element.37.refs_4_), custom_call_target="tpu_custom_call" | custom-call | flops 2717908992 | bytes 8388608 | tf_op jit(solution)/shard_map/filter/pallas_call | solution.py:262
  73.7 6.4 %filter.3 = bf16[32,8,16,256]{3,2,1,0:T(8,128)(2,1)} custom-call(f32[1,1]{1,0:T(1,128)} %bitcast.refs_0_, f32[1,8]{1,0:T(1,128)S(1)} %bitcast.13, bf16[32,2,128,256]{3,2,1,0:T(8,128)(2,1)S(1)} %get-tuple-element.32.refs_2_, bf16[32,2,128,256]{3,2,1,0:T(8,128)(2,1)S(1)} %get-tuple-element.36.refs_3_, bf16[2,216,768]{2,1,0:T(8,128)(2,1)S(1)} %get-tuple-element.37.refs_4_, ...), custom_call_target="tpu_custom_call" | custom-call | flops 2717908992 | bytes 8388608 | tf_op jit(solution)/shard_map/filter/pallas_call | solution.py:262
  (26 shorter events, 0.5 us)
Async XLA Ops:
  1.3 14.3 %collective-permute-start.1 = (bf16[4,16,16,256]{3,2,1,0:T(8,128)(2,1)S(1)}, bf16[4,16,16,256]{3,2,1,0:T(8,128)(2,1)S(1)}, u32[]{:S(2)}, u32[]{:S(2)}) collective-permute-start(bf16[4,16,16,256]{3,2,1,0:T(8,128)(2,1)S(1)} %get-tuple-element.44.refs_1_), channel_id=1, source_target_pairs={{0,2},{1,3},{2,0},{3,1},{4,6},{5,7},{6,4},{7,5},{8,10},{9,11},{10,... | collective-permute-start | bytes 1572872 | tf_op jit(solution)/shard_map/ppermute | solution.py:19
  9.3 0.8 %copy-start = (bf16[3,3,3,8,32]{4,3,2,1,0:T(8,128)(2,1)S(1)}, bf16[3,3,3,8,32]{4,3,2,1,0:T(8,128)(2,1)}, u32[]{:S(2)}) copy-start(bf16[3,3,3,8,32]{4,3,2,1,0:T(8,128)(2,1)} %param.16) | copy-start | bytes 41476
  10.7 4.9 %copy-start.2 = (bf16[32,16,256]{2,1,0:T(8,128)(2,1)S(1)}, bf16[32,16,256]{2,1,0:T(8,128)(2,1)}, u32[]{:S(2)}) copy-start(bf16[32,16,256]{2,1,0:T(8,128)(2,1)} %param.9) | copy-start | bytes 786436
  15.7 15.3 %collective-permute-start.3 = (bf16[4,16,16,256]{3,2,1,0:T(8,128)(2,1)S(1)}, bf16[4,16,16,256]{3,2,1,0:T(8,128)(2,1)S(1)}, u32[]{:S(2)}, u32[]{:S(2)}) collective-permute-start(bf16[4,16,16,256]{3,2,1,0:T(8,128)(2,1)S(1)} %collective-permute-done.1.refs_3_), channel_id=1, source_target_pairs={{0,4},{1,5},{4,8},{5,9},{6,2},{7,3},{8,12},{9,13},{10,6},{11,7},{1... | collective-permute-start | bytes 1572872 | tf_op jit(solution)/shard_map/ppermute | solution.py:19
  17.0 14.5 %collective-permute-start.5 = (bf16[4,16,16,256]{3,2,1,0:T(8,128)(2,1)S(1)}, bf16[4,16,16,256]{3,2,1,0:T(8,128)(2,1)S(1)}, u32[]{:S(2)}, u32[]{:S(2)}) collective-permute-start(bf16[4,16,16,256]{3,2,1,0:T(8,128)(2,1)S(1)} %get-tuple-element.43.refs_1_), channel_id=1, source_target_pairs={{0,2},{1,3},{2,0},{3,1},{4,6},{5,7},{6,4},{7,5},{8,10},{9,11},{10,... | collective-permute-start | bytes 1572872 | tf_op jit(solution)/shard_map/ppermute | solution.py:19
  19.0 12.6 %collective-permute-start = (bf16[4,16,16,256]{3,2,1,0:T(8,128)(2,1)S(1)}, bf16[4,16,16,256]{3,2,1,0:T(8,128)(2,1)S(1)}, u32[]{:S(2)}, u32[]{:S(2)}) collective-permute-start(bf16[4,16,16,256]{3,2,1,0:T(8,128)(2,1)S(1)} %get-tuple-element.44.refs_1_), channel_id=1, source_target_pairs={{0,1},{1,0},{2,3},{3,2},{4,5},{5,4},{6,7},{7,6},{8,9},{9,8},{10,11... | collective-permute-start | bytes 1572872 | tf_op jit(solution)/shard_map/ppermute | solution.py:19
  19.0 13.9 %collective-permute-start.2 = (bf16[4,16,16,256]{3,2,1,0:T(8,128)(2,1)S(1)}, bf16[4,16,16,256]{3,2,1,0:T(8,128)(2,1)S(1)}, u32[]{:S(2)}, u32[]{:S(2)}) collective-permute-start(bf16[4,16,16,256]{3,2,1,0:T(8,128)(2,1)S(1)} %collective-permute-done.1.refs_3_), channel_id=1, source_target_pairs={{0,1},{1,0},{2,3},{3,2},{4,5},{5,4},{6,7},{7,6},{8,9},{9,8},{10,11... | collective-permute-start | bytes 1572872 | tf_op jit(solution)/shard_map/ppermute | solution.py:19
  30.9 2.0 %collective-permute-start.4 = (bf16[4,16,16,256]{3,2,1,0:T(8,128)(2,1)S(1)}, bf16[4,16,16,256]{3,2,1,0:T(8,128)(2,1)S(1)}, u32[]{:S(2)}, u32[]{:S(2)}) collective-permute-start(bf16[4,16,16,256]{3,2,1,0:T(8,128)(2,1)S(1)} %collective-permute-done.3.refs_5_), channel_id=1, source_target_pairs={{0,1},{1,0},{2,3},{3,2},{4,5},{5,4},{6,7},{7,6},{8,9},{9,8},{10,11... | collective-permute-start | bytes 1572872 | tf_op jit(solution)/shard_map/ppermute | solution.py:19
  30.9 16.9 %collective-permute-start.8 = (bf16[4,16,16,256]{3,2,1,0:T(8,128)(2,1)S(1)}, bf16[4,16,16,256]{3,2,1,0:T(8,128)(2,1)S(1)}, u32[]{:S(2)}, u32[]{:S(2)}) collective-permute-start(bf16[4,16,16,256]{3,2,1,0:T(8,128)(2,1)S(1)} %get-tuple-element.43.refs_1_), channel_id=1, source_target_pairs={{0,1},{1,0},{2,3},{3,2},{4,5},{5,4},{6,7},{7,6},{8,9},{9,8},{10,11... | collective-permute-start | bytes 1572872 | tf_op jit(solution)/shard_map/ppermute | solution.py:19
  31.5 13.8 %collective-permute-start.7 = (bf16[4,16,16,256]{3,2,1,0:T(8,128)(2,1)S(1)}, bf16[4,16,16,256]{3,2,1,0:T(8,128)(2,1)S(1)}, u32[]{:S(2)}, u32[]{:S(2)}) collective-permute-start(bf16[4,16,16,256]{3,2,1,0:T(8,128)(2,1)S(1)} %collective-permute-done.5.refs_3_), channel_id=1, source_target_pairs={{0,1},{1,0},{2,3},{3,2},{4,5},{5,4},{6,7},{7,6},{8,9},{9,8},{10,11... | collective-permute-start | bytes 1572872 | tf_op jit(solution)/shard_map/ppermute | solution.py:19
  31.6 16.2 %collective-permute-start.6 = (bf16[4,16,16,256]{3,2,1,0:T(8,128)(2,1)S(1)}, bf16[4,16,16,256]{3,2,1,0:T(8,128)(2,1)S(1)}, u32[]{:S(2)}, u32[]{:S(2)}) collective-permute-start(bf16[4,16,16,256]{3,2,1,0:T(8,128)(2,1)S(1)} %collective-permute-done.5.refs_3_), channel_id=1, source_target_pairs={{0,4},{1,5},{4,8},{5,9},{6,2},{7,3},{8,12},{9,13},{10,6},{11,7},{1... | collective-permute-start | bytes 1572872 | tf_op jit(solution)/shard_map/ppermute | solution.py:19
  47.8 21.4 %copy-start.1 = (f32[8]{0:T(128)S(1)}, f32[8]{0:T(128)}, u32[]{:S(2)}) copy-start(f32[8]{0:T(128)} %param.17) | copy-start | bytes 100
  47.8 1.9 %collective-permute-start.9 = (bf16[4,16,16,256]{3,2,1,0:T(8,128)(2,1)S(1)}, bf16[4,16,16,256]{3,2,1,0:T(8,128)(2,1)S(1)}, u32[]{:S(2)}, u32[]{:S(2)}) collective-permute-start(bf16[4,16,16,256]{3,2,1,0:T(8,128)(2,1)S(1)} %collective-permute-done.6.refs_5_), channel_id=1, source_target_pairs={{0,1},{1,0},{2,3},{3,2},{4,5},{5,4},{6,7},{7,6},{8,9},{9,8},{10,11... | collective-permute-start | bytes 1572872 | tf_op jit(solution)/shard_map/ppermute | solution.py:19
  62.7 11.0 %collective-permute-start.10 = (bf16[256,256]{1,0:T(8,128)(2,1)S(1)}, bf16[256,256]{1,0:T(8,128)(2,1)S(1)}, u32[]{:S(2)}, u32[]{:S(2)}) collective-permute-start(bf16[256,256]{1,0:T(8,128)(2,1)S(1)} %get-tuple-element.41), channel_id=1, source_target_pairs={{0,1},{1,2},{2,3},{3,4},{4,5},{5,6},{6,7},{7,8},{8,9},{9,10},{10,1... | collective-permute-start | bytes 393224 | tf_op jit(solution)/shard_map/ppermute | solution.py:19
  64.7 8.9 %collective-permute-start.11 = (bf16[256,256]{1,0:T(8,128)(2,1)S(1)}, bf16[256,256]{1,0:T(8,128)(2,1)S(1)}, u32[]{:S(2)}, u32[]{:S(2)}) collective-permute-start(bf16[256,256]{1,0:T(8,128)(2,1)S(1)} %get-tuple-element.42), channel_id=1, source_target_pairs={{1,0},{2,1},{3,2},{4,3},{5,4},{6,5},{7,6},{8,7},{9,8},{10,9},{11,1... | collective-permute-start | bytes 393224 | tf_op jit(solution)/shard_map/ppermute | solution.py:19

commit v3 on v2

--- a/solution.py
+++ b/solution.py
@@ -6,9 +6,10 @@
 from jax.sharding import PartitionSpec as P
 
 MIB = 1024 * 1024
-CHUNKS = (16, 16)
+PARTS = ((8,), (12,), (12,))
+CHUNKS = tuple(sum(sizes) for sizes in PARTS)
 LANES = 128
-WIDE = 8
+WIDE = 16
 UNROLL = 4
 GROUP = 8
 
@@ -24,82 +25,124 @@
 
 
 def strip_offsets(tile):
-    low = (tile % 4) < 2
-    across = jnp.where(low, 2, -2)
-    along = -across
-    beside = jnp.where(tile % 2 == 0, 1, -1)
-    return jnp.stack([tile, tile + beside, tile + across, tile + beside + across, tile + along, tile + beside + along])
-
-
-def column_kernel(views, cols, tap_ref, frac_ref, out_ref):
+    across = jnp.where(lax.rem(tile, 4) < 2, 2, -2)
+    beside = jnp.where(lax.rem(tile, 2) == 0, 1, -1)
+    return [tile, tile + beside, tile + across, tile + beside + across, tile - across, tile + beside - across]
+
+
+def table_kernel(rows, tile_ref, count_ref, row_tap_ref, row_frac_ref, tap_ref, frac_ref, rowmat_ref, colmat_ref, taps, fracs):
+    views, planes, cols = tap_ref.shape
+    zero = jnp.zeros((), jnp.bfloat16)
+    tile = tile_ref[0, 0]
+    lane = lax.broadcasted_iota(jnp.int32, (rows, LANES), 1)
+    band = jnp.full((rows, LANES), -2, jnp.int32)
+    for slot, strip in enumerate(strip_offsets(tile)):
+        here = (lane >= slot * rows) & (lane < (slot + 1) * rows)
+        band = jnp.where(here, lane + (strip - slot) * rows, band)
+    for v in range(views):
+        scale = jnp.where(v < count_ref[0, 0], 1.0, 0.0)
+        for d in range(planes):
+            tap = row_tap_ref[v, :, d : d + 1]
+            frac = row_frac_ref[v, :, d : d + 1].astype(jnp.float32)
+            keep = 1.0 - frac
+            mat = jnp.where(band == tap, keep * scale, jnp.where(band == tap + 1, frac * scale, 0.0))
+            rowmat_ref[v, d * rows : (d + 1) * rows, :] = mat.astype(jnp.bfloat16)
+    taps[...] = tap_ref[...].astype(jnp.float32)
+    fracs[...] = frac_ref[...].astype(jnp.float32)
     index = lax.broadcasted_iota(jnp.int32, (cols, cols), 0).astype(jnp.bfloat16)
-    zero = jnp.zeros((), jnp.bfloat16)
 
     def plane(d, _):
         for v in range(views):
-            tap = tap_ref[v, pl.ds(d, 1), :]
-            frac = frac_ref[v, pl.ds(d, 1), :]
+            tap = taps[v, pl.ds(d, 1), :]
+            frac = fracs[v, pl.ds(d, 1), :]
             upper = jnp.where(index == (tap + 1.0).astype(jnp.bfloat16), frac.astype(jnp.bfloat16), zero)
-            out_ref[d, v] = jnp.where(index == tap.astype(jnp.bfloat16), (1.0 - frac).astype(jnp.bfloat16), upper)
+            colmat_ref[d, v] = jnp.where(index == tap.astype(jnp.bfloat16), (1.0 - frac).astype(jnp.bfloat16), upper)
         return 0
 
-    lax.fori_loop(0, tap_ref.shape[1], plane, 0)
-
-
-def column_matrices(tap, frac):
-    views, planes, cols = tap.shape
+    lax.fori_loop(0, planes, plane, 0)
+
+
+def tables(tile, view_count, row_tap, row_frac, col_tap, col_frac):
+    views, planes, cols = col_tap.shape
+    rows = row_tap.shape[2]
     vmem = pl.BlockSpec(memory_space=pltpu.VMEM)
+    smem = pl.BlockSpec(memory_space=pltpu.SMEM)
 
     def kernel(*refs):
-        column_kernel(views, cols, *refs)
+        table_kernel(rows, *refs)
 
     return pl.pallas_call(
         kernel,
-        out_shape=jax.ShapeDtypeStruct((planes, views, cols, cols), jnp.bfloat16),
-        in_specs=[vmem, vmem],
-        out_specs=vmem,
+        out_shape=(
+            jax.ShapeDtypeStruct((views, planes * rows, LANES), jnp.bfloat16),
+            jax.ShapeDtypeStruct((planes, views, cols, cols), jnp.bfloat16),
+        ),
+        in_specs=[smem, smem] + [vmem] * 4,
+        out_specs=(vmem, vmem),
+        scratch_shapes=[pltpu.VMEM((views, planes, cols), jnp.float32)] * 2,
         compiler_params=pltpu.CompilerParams(vmem_limit_bytes=20 * MIB),
-        name="columns",
-    )(tap, frac)
-
-
-def warp_kernel(strips, views, planes, chans, rows, cols, *refs):
+        name="tables",
+    )(
+        tile.reshape(1, 1).astype(jnp.int32),
+        view_count.reshape(1, 1),
+        jnp.swapaxes(row_tap, 1, 2),
+        jnp.swapaxes(row_frac, 1, 2),
+        col_tap,
+        col_frac,
+    )
+
+
+def warp_kernel(strips, sizes, views, planes, chans, rows, cols, *refs):
     inv_ref, refs = refs[0], refs[1:]
-    strip_refs, refs = refs[:strips], refs[strips:]
+    strip_refs, refs = refs[: strips * len(sizes)], refs[strips * len(sizes) :]
     base_ref, rowmat_ref, colmat_ref, var_ref, edge_ref, rowmix, even, odd = refs
     count = chans * rows
     half = rows // 2
     depth = rowmat_ref.shape[2]
-    wide = max(w for w in range(1, WIDE + 1) if chans % w == 0)
     blank = jnp.zeros((depth - strips * rows, cols), jnp.bfloat16)
 
-    def mix_rows(c, _):
-        for v in range(views):
-            bands = [
-                jnp.concatenate([s[v, c * wide + k] for s in strip_refs] + [blank], axis=0) for k in range(wide)
-            ]
-            band = jnp.concatenate(bands, axis=1)
-            for start in range(0, planes, 8):
-                lhs = rowmat_ref[v, start * rows : (start + 8) * rows, :]
-                mixed = jnp.dot(lhs, band, preferred_element_type=jnp.float32).astype(jnp.bfloat16)
-                for k in range(wide):
-                    at = pl.ds(pl.multiple_of((c * wide + k) * rows, rows), rows)
-                    rowmix[v, start : start + 8, at, :] = mixed[:, k * cols : (k + 1) * cols].reshape(8, rows, cols)
-        return 0
-
-    lax.fori_loop(0, chans // wide, mix_rows, 0)
+    def mix_rows(part, offset, wide, v, c):
+        refs_here = strip_refs[part :: len(sizes)]
+        bands = [
+            jnp.concatenate([ref[v, c * wide + k] for ref in refs_here] + [blank], axis=0) for k in range(wide)
+        ]
+        band = jnp.concatenate(bands, axis=1)
+        for start in range(0, planes, 8):
+            lhs = rowmat_ref[v, start * rows : (start + 8) * rows, :]
+            mixed = jnp.dot(lhs, band, preferred_element_type=jnp.float32).astype(jnp.bfloat16)
+            for k in range(wide):
+                at = pl.ds(pl.multiple_of((offset + c * wide + k) * rows, rows), rows)
+                rowmix[v, start : start + 8, at, :] = mixed[:, k * cols : (k + 1) * cols].reshape(8, rows, cols)
+
+    offset = 0
+    for part, size in enumerate(sizes):
+        wide = max(w for w in range(1, WIDE + 1) if size % w == 0)
+
+        def step(c, _, part=part, offset=offset, wide=wide):
+            for v in range(views):
+                mix_rows(part, offset, wide, v, c)
+            return 0
+
+        lax.fori_loop(0, size // wide, step, 0)
+        offset += size
     inv = inv_ref[0, 0]
 
+    held = views - 2
+
+    def warp_view(d, v):
+        return jnp.dot(rowmix[v, d], colmat_ref[d, v], preferred_element_type=jnp.float32)
+
     def warp_plane(d, warped):
-        for v in range(views):
-            warped[v] = jnp.dot(rowmix[v, d], colmat_ref[d, v], preferred_element_type=jnp.float32)
+        for v in range(held):
+            warped[v] = warp_view(d, v)
 
     def finish_plane(d, warped):
+        fresh = [warp_view(d, v) for v in range(held, views)]
         for c in range(0, chans, 2):
+            here = slice(c * rows, (c + 2) * rows)
             total = base_ref[c : c + 2].reshape(2 * rows, cols)
             squares = total * total
-            for v in range(views):
-                term = warped[v, c * rows : (c + 2) * rows, :]
+            for term in [warped[v, here, :] for v in range(held)] + [term[here] for term in fresh]:
                 total = total + term
                 squares = squares + term * term
             var = (squares - total * (total * inv)).reshape(2, 2, half, cols)
@@ -121,12 +164,14 @@
 
 
 def warp(inv, strips, base, rowmat, colmat):
-    views, size, rows, cols = strips[0].shape
+    views, _, rows, cols = strips[0][0].shape
+    sizes = [part.shape[1] for part in strips[0]]
+    size = sum(sizes)
     planes = colmat.shape[0]
     vmem = pl.BlockSpec(memory_space=pltpu.VMEM)
 
     def kernel(*refs):
-        warp_kernel(len(strips), views, planes, size, rows, cols, *refs)
+        warp_kernel(len(strips), sizes, views, planes, size, rows, cols, *refs)
 
     return pl.pallas_call(
         kernel,
@@ -134,7 +179,7 @@
             jax.ShapeDtypeStruct((planes, 2, size * rows // 2, cols), jnp.bfloat16),
             jax.ShapeDtypeStruct((2, planes, size, cols), jnp.float32),
         ),
-        in_specs=[pl.BlockSpec(memory_space=pltpu.SMEM)] + [vmem] * (len(strips) + 3),
+        in_specs=[pl.BlockSpec(memory_space=pltpu.SMEM)] + [vmem] * (len(strips) * len(sizes) + 3),
         out_specs=(vmem, vmem),
         scratch_shapes=[
             pltpu.VMEM((views, planes, size * rows, cols), jnp.bfloat16),
@@ -143,10 +188,10 @@
         ],
         compiler_params=pltpu.CompilerParams(vmem_limit_bytes=22 * MIB),
         cost_estimate=pl.CostEstimate(
-            flops=2 * views * planes * size * rows * cols * cols * 2, bytes_accessed=4 << 20, transcendentals=0
+            flops=1 << 20, bytes_accessed=1 << 10, transcendentals=0
         ),
         name="warp",
-    )(inv, *strips, base, rowmat, colmat)
+    )(inv, *[part for strip in strips for part in strip], base, rowmat, colmat)
 
 
 def joined_columns(terms, outs):
@@ -348,54 +393,44 @@
     ref_feat, src_feat, row_tap, row_frac, col_tap, col_frac, view_count, conv_weight, conv_bias
 ):
     rows = ref_feat.shape[1]
-    views = src_feat.shape[0]
-    planes = row_tap.shape[1]
     outs = conv_weight.shape[3]
     tile = lax.axis_index("tile")
 
-    starts = strip_offsets(tile) * rows
-    index = (starts[:, None] + jnp.arange(rows)).reshape(-1)
-    index = jnp.pad(index, (0, LANES - index.shape[0]), constant_values=-2)
-    keep = (1.0 - row_frac.astype(jnp.float32)).astype(jnp.bfloat16)
-    valid = (jnp.arange(views) < view_count[0])[:, None, None, None]
-    zero = jnp.zeros((), jnp.bfloat16)
-    rowmat = jnp.where(
-        (index == row_tap[..., None]) & valid,
-        keep[..., None],
-        jnp.where((index == row_tap[..., None] + 1) & valid, row_frac[..., None], zero),
-    ).reshape(views, planes * rows, -1)
     inv = (1.0 / (1.0 + view_count.astype(jnp.float32))).reshape(1, 1)
-    frac = col_frac.astype(jnp.float32)
-    colmat = column_matrices(col_tap.astype(jnp.float32), frac)
-    base = ref_feat.astype(jnp.float32)
-    filter_mat, edge_mat = matrices(conv_weight, rows, CHUNKS, GROUP)
-
-    spans = [slice(sum(CHUNKS[:i]), sum(CHUNKS[: i + 1])) for i in range(len(CHUNKS))]
-    pieces = [src_feat[:, span] for span in spans]
+    rowmat, colmat = tables(tile, view_count, row_tap, row_frac, col_tap, col_frac)
+
+    sizes = [size for chunk in PARTS for size in chunk]
+    pieces = [src_feat[:, sum(sizes[:i]) : sum(sizes[: i + 1])] for i in range(len(sizes))]
     pieces[1:] = lax.optimization_barrier(pieces[1:])
     across = [routed(piece, lambda i: i ^ 2) for piece in pieces]
     beside = [routed(piece, lambda i: i ^ 1) for piece in pieces]
-    bases = [base[span] for span in spans]
-    across[0], rowmat, colmat, bases, filter_mat, edge_mat = lax.optimization_barrier(
-        (across[0], rowmat, colmat, bases, filter_mat, edge_mat)
+    across[0], rowmat, colmat, ref_feat, conv_weight = lax.optimization_barrier(
+        (across[0], rowmat, colmat, ref_feat, conv_weight)
     )
+    along = [routed(across[0], onward)]
+    base = ref_feat.astype(jnp.float32)
+    bases = [base[sum(CHUNKS[:i]) : sum(CHUNKS[: i + 1])] for i in range(len(CHUNKS))]
+    filter_mat, edge_mat = matrices(conv_weight, rows, CHUNKS, GROUP)
     variances = []
     edges = []
-    along = routed(across[0], onward)
-    across_beside = routed(across[0], lambda i: i ^ 1)
-    for i in range(len(CHUNKS)):
-        along_beside = routed(along, lambda i: i ^ 1)
-        strips = [pieces[i], beside[i], across[i], across_beside, along, along_beside]
-        if i + 1 < len(CHUNKS):
-            along = routed(across[i + 1], onward)
-            across_beside = routed(across[i + 1], lambda i: i ^ 1)
+    begin = 0
+    across_beside = []
+    for i, chunk in enumerate(PARTS):
+        end = begin + len(chunk)
+        ahead = end + (len(PARTS[i + 1]) if i + 1 < len(PARTS) else 0)
+        along += [routed(part, onward) for part in across[len(along) : ahead]]
+        across_beside += [routed(part, lambda i: i ^ 1) for part in across[len(across_beside) : ahead]]
+        here = slice(begin, end)
+        along_beside = [routed(part, lambda i: i ^ 1) for part in along[here]]
+        strips = [pieces[here], beside[here], across[here], across_beside[here], along[here], along_beside]
         var, edge = warp(inv, strips, bases[i], rowmat, colmat)
-        if i + 1 < len(CHUNKS):
-            var, edge, along, across_beside, across[i + 2 :] = lax.optimization_barrier(
-                (var, edge, along, across_beside, across[i + 2 :])
+        if i + 1 < len(PARTS):
+            var, edge, along[end:], across_beside[end:], across[ahead:] = lax.optimization_barrier(
+                (var, edge, along[end:], across_beside[end:], across[ahead:])
             )
         variances.append(var)
         edges.append(edge)
+        begin = end
     up, down = edge_terms(inv, edges, edge_mat, outs)
     above = routed(down, lambda i: i + 1)
     below = routed(up, lambda i: i - 1)

time: 81.4 us -> 76 us (0.934)
  waiting for transfers between devices: 15.8 us -> 7.87 us
  other arithmetic: 4.77 us -> 0 us
  starting transfers between devices: 13.8 us -> 17.2 us
  Pallas kernels: 40.2 us -> 42.5 us
  local copies, waits for them, and re-layouts: 4.55 us -> 6.25 us
    ppermute x12 -> x17, waiting for transfers between devices: 15.8 us -> 7.87 us  [routed(): return lax.ppermute(x, 'tile', pairs)]
    ppermute x12 -> x17, starting transfers between devices: 13.8 us -> 17.2 us  [routed(): return lax.ppermute(x, 'tile', pairs)]
    convert_element_type x3 -> x0, other arithmetic: 2.5 us -> none  [the longest x1 0.92 us: on_device(): colmat = column_matrices(col_tap.astype(jnp.float32), frac)]
    slice x2 -> x4, local copies, waits for them, and re-layouts: 1.35 us -> 3.02 us  [the longest x2 2.13 us: on_device(): src_feat[:, sum(sizes[:i]):sum(sizes[:i + 1])]]
    select_n x1 -> x0, other arithmetic: 1.43 us -> none  [on_device(): jnp.where((index == row_tap[..., None]) & valid, keep[..., None], jnp.whe...]
    pallas_call x2 -> x3, Pallas kernels: 24.8 us -> 25.9 us  [warp(): pl.pallas_call(kernel, out_shape=(jax.ShapeDtypeStruct((planes, 2, size *...]
    pallas_call x1, Pallas kernels: 3.4 us -> 4.47 us  [tables(): pl.pallas_call(kernel, out_shape=(jax.ShapeDtypeStruct((views, planes * r...]
    add x2 -> x0, other arithmetic: 0.83 us -> none  [the longest x1 0.76 us: on_device(): row_tap[..., None] + 1]
  transfers between devices with their start and end apart: 12 -> 17, of which waited for: 3 -> 4; matrix products, arithmetic and copies ran while one was open for 9% -> 3% of each run, Pallas kernels for 26% -> 35%
where the time goes in v3:
time: 76 us; the launch traced here: 74.8 us
  Pallas kernels  42.5 us (56%)
  starting transfers between devices  17.2 us (23%)
  waiting for transfers between devices  7.87 us (10%)
  local copies, waits for them, and re-layouts  6.25 us (8%)
  between operations  0.95 us (1%)
    pallas_call x3, Pallas kernels, warp(): pl.pallas_call(kernel, out_shape=(jax.ShapeDtypeStruct((planes, 2, size *...  25.9 us
    ppermute x17, starting transfers between devices, routed(): return lax.ppermute(x, 'tile', pairs)  17.2 us
    pallas_call x2, Pallas kernels, filtered(): pl.pallas_call(kernel, out_shape=jax.ShapeDtypeStruct((count, rows * outs...  10.9 us
    ppermute x17, waiting for transfers between devices, routed(): return lax.ppermute(x, 'tile', pairs)  7.87 us
    pallas_call x1, Pallas kernels, tables(): pl.pallas_call(kernel, out_shape=(jax.ShapeDtypeStruct((views, planes * r...  4.47 us
    unnamed x14, local copies, waits for them, and re-layouts  3.23 us
    slice x2, local copies, waits for them, and re-layouts, on_device(): src_feat[:, sum(sizes[:i]):sum(sizes[:i + 1])]  2.13 us
  transfers between devices with their start and end apart: 17, of which 4 were waited for; matrix products, arithmetic and copies ran while one was open for 3% of the time, Pallas kernels for 35%

profile of v3, /device:TPU:24, one launch (start us, length us, event | category | flops | bytes accessed | tf_op | source)
XLA Modules:
  0.0 74.8 jit_solution(8314352900683511500)
XLA Ops:
  0.0 1.0 %slice.18.refs_1_ = bf16[4,8,16,256]{3,2,1,0:T(8,128)(2,1)S(1)} slice(bf16[4,32,16,256]{3,2,1,0:T(8,128)(2,1)} %param.10), slice={[0:4], [0:8], [0:16], [0:256]} | slice | bytes 524288 | tf_op jit(solution)/shard_map/slice | solution.py:403
  1.0 1.6 %collective-permute-start.1 = (bf16[4,8,16,256]{3,2,1,0:T(8,128)(2,1)S(1)}, bf16[4,8,16,256]{3,2,1,0:T(8,128)(2,1)S(1)}, u32[]{:S(2)}, u32[]{:S(2)}) collective-permute-start(bf16[4,8,16,256]{3,2,1,0:T(8,128)(2,1)S(1)} %slice.18.refs_1_), channel_id=1, source_target_pairs={{0,2},{1,3},{2,0},{3,1},{4,6},{5,7},{6,4},{7,5},{8,10},{9,11},{10,... | collective-permute-start | bytes 786440 | tf_op jit(solution)/shard_map/ppermute | solution.py:20
  2.6 1.2 %fusion = (bf16[4,12,16,256]{3,2,1,0:T(8,128)(2,1)S(1)}, bf16[4,12,16,256]{3,2,1,0:T(8,128)(2,1)S(1)}) fusion(bf16[4,32,16,256]{3,2,1,0:T(8,128)(2,1)} %param.10), kind=kLoop, calls=%fused_computation | loop fusion | bytes 1572864 | tf_op jit(solution)/shard_map/slice | solution.py:403
  3.7 0.6 collective-permute-start.5
  5.0 0.9 %copy-done = s32[4,32,256]{2,1,0:T(8,128)S(1)} copy-done((s32[4,32,256]{2,1,0:T(8,128)S(1)}, s32[4,32,256]{2,1,0:T(8,128)}, u32[]{:S(2)}) %copy-start) | copy-done | bytes 131096
  5.9 0.8 %copy-done.1 = bf16[4,32,256]{2,1,0:T(8,128)(2,1)S(1)} copy-done((bf16[4,32,256]{2,1,0:T(8,128)(2,1)S(1)}, bf16[4,32,256]{2,1,0:T(8,128)(2,1)}, u32[]{:S(2)}) %copy-start.1) | copy-done | bytes 65560
  6.7 0.8 %copy-done.3 = s32[4,32,16]{1,2,0:T(8,128)S(1)} copy-done((s32[4,32,16]{1,2,0:T(8,128)S(1)}, s32[4,32,16]{1,2,0:T(8,128)}, u32[]{:S(2)}) %copy-start.3) | copy-done | bytes 8216
  7.5 0.7 copy-done.4
  8.2 4.5 %tables.1 = (bf16[4,512,128]{2,1,0:T(8,128)(2,1)S(1)}, bf16[32,4,256,256]{3,2,1,0:T(8,128)(2,1)S(1)}) custom-call(s32[1,1]{1,0:T(1,128)} %bitcast.2.refs_0_, s32[1,1]{1,0:T(1,128)} %bitcast.7.refs_1_, s32[4,16,32]{2,1,0:T(8,128)S(1)} %bitcast.9, bf16[4,16,32]{2,1,0:T(8,128)(2,1)S(1)} %bitcast.10, s32[4,32,256]{2,1,0:T(8,128)S(1)} %copy-done, ...), custom_call_target="tpu_custom_call" | custom-call | tf_op jit(solution)/shard_map/tables/pallas_call | solution.py:74
  12.7 1.3 %collective-permute-start.3 = (bf16[4,8,16,256]{3,2,1,0:T(8,128)(2,1)S(1)}, bf16[4,8,16,256]{3,2,1,0:T(8,128)(2,1)S(1)}, u32[]{:S(2)}, u32[]{:S(2)}) collective-permute-start(bf16[4,8,16,256]{3,2,1,0:T(8,128)(2,1)S(1)} %collective-permute-done.1.refs_3_), channel_id=1, source_target_pairs={{0,4},{1,5},{4,8},{5,9},{6,2},{7,3},{8,12},{9,13},{10,6},{11,7},{1... | collective-permute-start | bytes 786440 | tf_op jit(solution)/shard_map/ppermute | solution.py:20
  14.0 2.7 %collective-permute-start.8 = (bf16[4,12,16,256]{3,2,1,0:T(8,128)(2,1)S(1)}, bf16[4,12,16,256]{3,2,1,0:T(8,128)(2,1)S(1)}, u32[]{:S(2)}, u32[]{:S(2)}) collective-permute-start(bf16[4,12,16,256]{3,2,1,0:T(8,128)(2,1)S(1)} %get-tuple-element.42.refs_1_), channel_id=1, source_target_pairs={{0,2},{1,3},{2,0},{3,1},{4,6},{5,7},{6,4},{7,5},{8,10},{9,11},{10,... | collective-permute-start | bytes 1179656 | tf_op jit(solution)/shard_map/ppermute | solution.py:20
  16.6 0.9 %collective-permute-done.5.refs_3_ = bf16[4,12,16,256]{3,2,1,0:T(8,128)(2,1)S(1)} collective-permute-done((bf16[4,12,16,256]{3,2,1,0:T(8,128)(2,1)S(1)}, bf16[4,12,16,256]{3,2,1,0:T(8,128)(2,1)S(1)}, u32[]{:S(2)}, u32[]{:S(2)}) %collective-permute-start.5) | collective-permute-done | bytes 393248 | tf_op jit(solution)/shard_map/ppermute | solution.py:20
  17.5 1.3 %collective-permute-start.6 = (bf16[4,12,16,256]{3,2,1,0:T(8,128)(2,1)S(1)}, bf16[4,12,16,256]{3,2,1,0:T(8,128)(2,1)S(1)}, u32[]{:S(2)}, u32[]{:S(2)}) collective-permute-start(bf16[4,12,16,256]{3,2,1,0:T(8,128)(2,1)S(1)} %collective-permute-done.5.refs_3_), channel_id=1, source_target_pairs={{0,4},{1,5},{4,8},{5,9},{6,2},{7,3},{8,12},{9,13},{10,6},{11,7},{1... | collective-permute-start | bytes 1179656 | tf_op jit(solution)/shard_map/ppermute | solution.py:20
  18.9 0.5 collective-permute-start.2
  19.4 4.3 %collective-permute-done.3.refs_5_ = bf16[4,8,16,256]{3,2,1,0:T(8,128)(2,1)S(1)} collective-permute-done((bf16[4,8,16,256]{3,2,1,0:T(8,128)(2,1)S(1)}, bf16[4,8,16,256]{3,2,1,0:T(8,128)(2,1)S(1)}, u32[]{:S(2)}, u32[]{:S(2)}) %collective-permute-start.3) | collective-permute-done | bytes 262176 | tf_op jit(solution)/shard_map/ppermute | solution.py:20
  23.7 0.9 %slice.24.refs_7_ = f32[8,16,256]{2,1,0:T(8,128)S(1)} slice(bf16[32,16,256]{2,1,0:T(8,128)(2,1)} %param.9), slice={[0:8], [0:16], [0:256]} | slice | bytes 262144 | tf_op jit(solution)/shard_map/slice | solution.py:412
  24.6 0.6 collective-permute-start.9
  25.2 6.7 %warp.3 = (bf16[32,2,64,256]{3,2,1,0:T(8,128)(2,1)S(1)}, f32[2,32,8,256]{3,2,1,0:T(8,128)S(1)}) custom-call(f32[1,1]{1,0:T(1,128)} %bitcast.refs_0_, bf16[4,8,16,256]{3,2,1,0:T(8,128)(2,1)S(1)} %slice.18.refs_1_, bf16[4,8,16,256]{3,2,1,0:T(8,128)(2,1)S(1)} %collective-permute-done.refs_2_, bf16[4,8,16,256]{3,2,1,0:T(8,128)(2,1)S(1)} %collective-permute-done.1.refs_3_, ...), custom_call_target="tpu_custom_call" | custom-call | flops 1048576 | bytes 1024 | tf_op jit(solution)/shard_map/warp/pallas_call | solution.py:176
  32.0 0.2 collective-permute-start.10
  32.2 1.5 %collective-permute-start.11 = (bf16[4,12,16,256]{3,2,1,0:T(8,128)(2,1)S(1)}, bf16[4,12,16,256]{3,2,1,0:T(8,128)(2,1)S(1)}, u32[]{:S(2)}, u32[]{:S(2)}) collective-permute-start(bf16[4,12,16,256]{3,2,1,0:T(8,128)(2,1)S(1)} %collective-permute-done.8.refs_3_), channel_id=1, source_target_pairs={{0,4},{1,5},{4,8},{5,9},{6,2},{7,3},{8,12},{9,13},{10,6},{11,7},{1... | collective-permute-start | bytes 1179656 | tf_op jit(solution)/shard_map/ppermute | solution.py:20
  33.6 0.4 collective-permute-start.12
  34.1 0.1 collective-permute-start.13
  34.3 9.6 %warp.4 = (bf16[32,2,96,256]{3,2,1,0:T(8,128)(2,1)S(1)}, f32[2,32,12,256]{3,2,1,0:T(8,128)S(1)}) custom-call(f32[1,1]{1,0:T(1,128)} %bitcast.refs_0_, bf16[4,12,16,256]{3,2,1,0:T(8,128)(2,1)S(1)} %get-tuple-element.41.refs_1_, bf16[4,12,16,256]{3,2,1,0:T(8,128)(2,1)S(1)} %collective-permute-done.9.refs_2_, ...), custom_call_target="tpu_custom_call" | custom-call | flops 1048576 | bytes 1024 | tf_op jit(solution)/shard_map/warp/pallas_call | solution.py:176
  43.9 1.5 %collective-permute-done.11.refs_5_ = bf16[4,12,16,256]{3,2,1,0:T(8,128)(2,1)S(1)} collective-permute-done((bf16[4,12,16,256]{3,2,1,0:T(8,128)(2,1)S(1)}, bf16[4,12,16,256]{3,2,1,0:T(8,128)(2,1)S(1)}, u32[]{:S(2)}, u32[]{:S(2)}) %collective-permute-start.11) | collective-permute-done | bytes 393248 | tf_op jit(solution)/shard_map/ppermute | solution.py:20
  45.5 0.6 matrices.1
  46.1 1.1 %collective-permute-done.14.refs_6_ = bf16[4,12,16,256]{3,2,1,0:T(8,128)(2,1)S(1)} collective-permute-done((bf16[4,12,16,256]{3,2,1,0:T(8,128)(2,1)S(1)}, bf16[4,12,16,256]{3,2,1,0:T(8,128)(2,1)S(1)}, u32[]{:S(2)}, u32[]{:S(2)}) %collective-permute-start.14) | collective-permute-done | bytes 393248 | tf_op jit(solution)/shard_map/ppermute | solution.py:20
  47.2 9.6 %warp.5 = (bf16[32,2,96,256]{3,2,1,0:T(8,128)(2,1)S(1)}, f32[2,32,12,256]{3,2,1,0:T(8,128)S(1)}) custom-call(f32[1,1]{1,0:T(1,128)} %bitcast.refs_0_, bf16[4,12,16,256]{3,2,1,0:T(8,128)(2,1)S(1)} %get-tuple-element.42.refs_1_, bf16[4,12,16,256]{3,2,1,0:T(8,128)(2,1)S(1)} %collective-permute-done.13.refs_2_, ...), custom_call_target="tpu_custom_call" | custom-call | flops 1048576 | bytes 1024 | tf_op jit(solution)/shard_map/warp/pallas_call | solution.py:176
  56.8 0.6 edge.1
  57.4 2.0 %collective-permute-start.15 = (bf16[256,256]{1,0:T(8,128)(2,1)S(1)}, bf16[256,256]{1,0:T(8,128)(2,1)S(1)}, u32[]{:S(2)}, u32[]{:S(2)}) collective-permute-start(bf16[256,256]{1,0:T(8,128)(2,1)S(1)} %get-tuple-element.59), channel_id=1, source_target_pairs={{0,1},{1,2},{2,3},{3,4},{4,5},{5,6},{6,7},{7,8},{8,9},{9,10},{10,1... | collective-permute-start | bytes 393224 | tf_op jit(solution)/shard_map/ppermute | solution.py:20
  59.4 4.4 %collective-permute-start.16 = (bf16[256,256]{1,0:T(8,128)(2,1)S(1)}, bf16[256,256]{1,0:T(8,128)(2,1)S(1)}, u32[]{:S(2)}, u32[]{:S(2)}) collective-permute-start(bf16[256,256]{1,0:T(8,128)(2,1)S(1)} %get-tuple-element.60), channel_id=1, source_target_pairs={{1,0},{2,1},{3,2},{4,3},{5,4},{6,5},{7,6},{8,7},{9,8},{10,9},{11,1... | collective-permute-start | bytes 393224 | tf_op jit(solution)/shard_map/ppermute | solution.py:20
  63.9 4.5 %filter.2.refs_6_ = f32[16,128,256]{2,1,0:T(8,128)S(1)} custom-call(f32[1,1]{1,0:T(1,128)} %bitcast.refs_0_, f32[1,8]{1,0:T(1,128)S(1)} %bitcast.11, bf16[32,2,64,256]{3,2,1,0:T(8,128)(2,1)S(1)} %get-tuple-element.43.refs_2_, bf16[32,2,96,256]{3,2,1,0:T(8,128)(2,1)S(1)} %get-tuple-element.49.refs_3_, bf16[32,2,96,256]{3,2,1,0:T(8,128)(2,1)S(1)} %get-tuple-element.52.refs_4_, ...), custom_call_target="tpu_custom_call" | custom-call | flops 2717908992 | bytes 8388608 | tf_op jit(solution)/shard_map/filter/pallas_call | solution.py:307
  68.4 6.4 %filter.3 = bf16[32,8,16,256]{3,2,1,0:T(8,128)(2,1)} custom-call(f32[1,1]{1,0:T(1,128)} %bitcast.refs_0_, f32[1,8]{1,0:T(1,128)S(1)} %bitcast.12, bf16[32,2,64,256]{3,2,1,0:T(8,128)(2,1)S(1)} %get-tuple-element.43.refs_2_, bf16[32,2,96,256]{3,2,1,0:T(8,128)(2,1)S(1)} %get-tuple-element.49.refs_3_, bf16[32,2,96,256]{3,2,1,0:T(8,128)(2,1)S(1)} %get-tuple-element.52.refs_4_, ...), custom_call_target="tpu_custom_call" | custom-call | flops 2717908992 | bytes 8388608 | tf_op jit(solution)/shard_map/filter/pallas_call | solution.py:307
  (28 shorter events, 0.2 us)
Async XLA Ops:
  1.0 11.7 %collective-permute-start.1 = (bf16[4,8,16,256]{3,2,1,0:T(8,128)(2,1)S(1)}, bf16[4,8,16,256]{3,2,1,0:T(8,128)(2,1)S(1)}, u32[]{:S(2)}, u32[]{:S(2)}) collective-permute-start(bf16[4,8,16,256]{3,2,1,0:T(8,128)(2,1)S(1)} %slice.18.refs_1_), channel_id=1, source_target_pairs={{0,2},{1,3},{2,0},{3,1},{4,6},{5,7},{6,4},{7,5},{8,10},{9,11},{10,... | collective-permute-start | bytes 786440 | tf_op jit(solution)/shard_map/ppermute | solution.py:20
  3.7 13.8 %collective-permute-start.5 = (bf16[4,12,16,256]{3,2,1,0:T(8,128)(2,1)S(1)}, bf16[4,12,16,256]{3,2,1,0:T(8,128)(2,1)S(1)}, u32[]{:S(2)}, u32[]{:S(2)}) collective-permute-start(bf16[4,12,16,256]{3,2,1,0:T(8,128)(2,1)S(1)} %get-tuple-element.41.refs_1_), channel_id=1, source_target_pairs={{0,2},{1,3},{2,0},{3,1},{4,6},{5,7},{6,4},{7,5},{8,10},{9,11},{10,... | collective-permute-start | bytes 1179656 | tf_op jit(solution)/shard_map/ppermute | solution.py:20
  4.3 14.6 %collective-permute-start = (bf16[4,8,16,256]{3,2,1,0:T(8,128)(2,1)S(1)}, bf16[4,8,16,256]{3,2,1,0:T(8,128)(2,1)S(1)}, u32[]{:S(2)}, u32[]{:S(2)}) collective-permute-start(bf16[4,8,16,256]{3,2,1,0:T(8,128)(2,1)S(1)} %slice.18.refs_1_), channel_id=1, source_target_pairs={{0,1},{1,0},{2,3},{3,2},{4,5},{5,4},{6,7},{7,6},{8,9},{9,8},{10,11... | collective-permute-start | bytes 786440 | tf_op jit(solution)/shard_map/ppermute | solution.py:20
  5.0 0.9 %copy-start = (s32[4,32,256]{2,1,0:T(8,128)S(1)}, s32[4,32,256]{2,1,0:T(8,128)}, u32[]{:S(2)}) copy-start(s32[4,32,256]{2,1,0:T(8,128)} %refs_4_.1) | copy-start | bytes 393220
  5.9 0.8 %copy-start.1 = (bf16[4,32,256]{2,1,0:T(8,128)(2,1)S(1)}, bf16[4,32,256]{2,1,0:T(8,128)(2,1)}, u32[]{:S(2)}) copy-start(bf16[4,32,256]{2,1,0:T(8,128)(2,1)} %refs_5_.1) | copy-start | bytes 196612
  6.7 0.8 %copy-start.3 = (s32[4,32,16]{1,2,0:T(8,128)S(1)}, s32[4,32,16]{1,2,0:T(8,128)}, u32[]{:S(2)}) copy-start(s32[4,32,16]{1,2,0:T(8,128)} %param.11) | copy-start | bytes 24580
  7.5 0.7 copy-start.4
  12.7 11.0 %collective-permute-start.3 = (bf16[4,8,16,256]{3,2,1,0:T(8,128)(2,1)S(1)}, bf16[4,8,16,256]{3,2,1,0:T(8,128)(2,1)S(1)}, u32[]{:S(2)}, u32[]{:S(2)}) collective-permute-start(bf16[4,8,16,256]{3,2,1,0:T(8,128)(2,1)S(1)} %collective-permute-done.1.refs_3_), channel_id=1, source_target_pairs={{0,4},{1,5},{4,8},{5,9},{6,2},{7,3},{8,12},{9,13},{10,6},{11,7},{1... | collective-permute-start | bytes 786440 | tf_op jit(solution)/shard_map/ppermute | solution.py:20
  14.0 18.0 %collective-permute-start.8 = (bf16[4,12,16,256]{3,2,1,0:T(8,128)(2,1)S(1)}, bf16[4,12,16,256]{3,2,1,0:T(8,128)(2,1)S(1)}, u32[]{:S(2)}, u32[]{:S(2)}) collective-permute-start(bf16[4,12,16,256]{3,2,1,0:T(8,128)(2,1)S(1)} %get-tuple-element.42.refs_1_), channel_id=1, source_target_pairs={{0,2},{1,3},{2,0},{3,1},{4,6},{5,7},{6,4},{7,5},{8,10},{9,11},{10,... | collective-permute-start | bytes 1179656 | tf_op jit(solution)/shard_map/ppermute | solution.py:20
  17.5 14.4 %collective-permute-start.6 = (bf16[4,12,16,256]{3,2,1,0:T(8,128)(2,1)S(1)}, bf16[4,12,16,256]{3,2,1,0:T(8,128)(2,1)S(1)}, u32[]{:S(2)}, u32[]{:S(2)}) collective-permute-start(bf16[4,12,16,256]{3,2,1,0:T(8,128)(2,1)S(1)} %collective-permute-done.5.refs_3_), channel_id=1, source_target_pairs={{0,4},{1,5},{4,8},{5,9},{6,2},{7,3},{8,12},{9,13},{10,6},{11,7},{1... | collective-permute-start | bytes 1179656 | tf_op jit(solution)/shard_map/ppermute | solution.py:20
  18.8 13.2 %collective-permute-start.7 = (bf16[4,12,16,256]{3,2,1,0:T(8,128)(2,1)S(1)}, bf16[4,12,16,256]{3,2,1,0:T(8,128)(2,1)S(1)}, u32[]{:S(2)}, u32[]{:S(2)}) collective-permute-start(bf16[4,12,16,256]{3,2,1,0:T(8,128)(2,1)S(1)} %collective-permute-done.5.refs_3_), channel_id=1, source_target_pairs={{0,1},{1,0},{2,3},{3,2},{4,5},{5,4},{6,7},{7,6},{8,9},{9,8},{10,11... | collective-permute-start | bytes 1179656 | tf_op jit(solution)/shard_map/ppermute | solution.py:20
  18.9 5.7 %collective-permute-start.2 = (bf16[4,8,16,256]{3,2,1,0:T(8,128)(2,1)S(1)}, bf16[4,8,16,256]{3,2,1,0:T(8,128)(2,1)S(1)}, u32[]{:S(2)}, u32[]{:S(2)}) collective-permute-start(bf16[4,8,16,256]{3,2,1,0:T(8,128)(2,1)S(1)} %collective-permute-done.1.refs_3_), channel_id=1, source_target_pairs={{0,1},{1,0},{2,3},{3,2},{4,5},{5,4},{6,7},{7,6},{8,9},{9,8},{10,11... | collective-permute-start | bytes 786440 | tf_op jit(solution)/shard_map/ppermute | solution.py:20
  23.7 1.5 %collective-permute-start.4 = (bf16[4,8,16,256]{3,2,1,0:T(8,128)(2,1)S(1)}, bf16[4,8,16,256]{3,2,1,0:T(8,128)(2,1)S(1)}, u32[]{:S(2)}, u32[]{:S(2)}) collective-permute-start(bf16[4,8,16,256]{3,2,1,0:T(8,128)(2,1)S(1)} %collective-permute-done.3.refs_5_), channel_id=1, source_target_pairs={{0,1},{1,0},{2,3},{3,2},{4,5},{5,4},{6,7},{7,6},{8,9},{9,8},{10,11... | collective-permute-start | bytes 786440 | tf_op jit(solution)/shard_map/ppermute | solution.py:20
  24.6 9.7 %collective-permute-start.9 = (bf16[4,12,16,256]{3,2,1,0:T(8,128)(2,1)S(1)}, bf16[4,12,16,256]{3,2,1,0:T(8,128)(2,1)S(1)}, u32[]{:S(2)}, u32[]{:S(2)}) collective-permute-start(bf16[4,12,16,256]{3,2,1,0:T(8,128)(2,1)S(1)} %get-tuple-element.41.refs_1_), channel_id=1, source_target_pairs={{0,1},{1,0},{2,3},{3,2},{4,5},{5,4},{6,7},{7,6},{8,9},{9,8},{10,11... | collective-permute-start | bytes 1179656 | tf_op jit(solution)/shard_map/ppermute | solution.py:20
  25.2 9.0 %copy-start.6 = (bf16[32,16,256]{2,1,0:T(8,128)(2,1)S(1)}, bf16[32,16,256]{2,1,0:T(8,128)(2,1)}, u32[]{:S(2)}) copy-start(bf16[32,16,256]{2,1,0:T(8,128)(2,1)} %param.9) | copy-start | bytes 786436
  32.0 2.3 %collective-permute-start.10 = (bf16[4,12,16,256]{3,2,1,0:T(8,128)(2,1)S(1)}, bf16[4,12,16,256]{3,2,1,0:T(8,128)(2,1)S(1)}, u32[]{:S(2)}, u32[]{:S(2)}) collective-permute-start(bf16[4,12,16,256]{3,2,1,0:T(8,128)(2,1)S(1)} %collective-permute-done.6.refs_5_), channel_id=1, source_target_pairs={{0,1},{1,0},{2,3},{3,2},{4,5},{5,4},{6,7},{7,6},{8,9},{9,8},{10,11... | collective-permute-start | bytes 1179656 | tf_op jit(solution)/shard_map/ppermute | solution.py:20
  32.2 13.3 %collective-permute-start.11 = (bf16[4,12,16,256]{3,2,1,0:T(8,128)(2,1)S(1)}, bf16[4,12,16,256]{3,2,1,0:T(8,128)(2,1)S(1)}, u32[]{:S(2)}, u32[]{:S(2)}) collective-permute-start(bf16[4,12,16,256]{3,2,1,0:T(8,128)(2,1)S(1)} %collective-permute-done.8.refs_3_), channel_id=1, source_target_pairs={{0,4},{1,5},{4,8},{5,9},{6,2},{7,3},{8,12},{9,13},{10,6},{11,7},{1... | collective-permute-start | bytes 1179656 | tf_op jit(solution)/shard_map/ppermute | solution.py:20
  33.6 11.8 %collective-permute-start.12 = (bf16[4,12,16,256]{3,2,1,0:T(8,128)(2,1)S(1)}, bf16[4,12,16,256]{3,2,1,0:T(8,128)(2,1)S(1)}, u32[]{:S(2)}, u32[]{:S(2)}) collective-permute-start(bf16[4,12,16,256]{3,2,1,0:T(8,128)(2,1)S(1)} %collective-permute-done.8.refs_3_), channel_id=1, source_target_pairs={{0,1},{1,0},{2,3},{3,2},{4,5},{5,4},{6,7},{7,6},{8,9},{9,8},{10,11... | collective-permute-start | bytes 1179656 | tf_op jit(solution)/shard_map/ppermute | solution.py:20
  34.1 12.0 %collective-permute-start.13 = (bf16[4,12,16,256]{3,2,1,0:T(8,128)(2,1)S(1)}, bf16[4,12,16,256]{3,2,1,0:T(8,128)(2,1)S(1)}, u32[]{:S(2)}, u32[]{:S(2)}) collective-permute-start(bf16[4,12,16,256]{3,2,1,0:T(8,128)(2,1)S(1)} %get-tuple-element.42.refs_1_), channel_id=1, source_target_pairs={{0,1},{1,0},{2,3},{3,2},{4,5},{5,4},{6,7},{7,6},{8,9},{9,8},{10,11... | collective-permute-start | bytes 1179656 | tf_op jit(solution)/shard_map/ppermute | solution.py:20
  34.3 11.2 %copy-start.2 = (bf16[3,3,3,8,32]{4,3,2,1,0:T(8,128)(2,1)S(1)}, bf16[3,3,3,8,32]{4,3,2,1,0:T(8,128)(2,1)}, u32[]{:S(2)}) copy-start(bf16[3,3,3,8,32]{4,3,2,1,0:T(8,128)(2,1)} %param.16) | copy-start | bytes 41476
  45.5 1.7 %collective-permute-start.14 = (bf16[4,12,16,256]{3,2,1,0:T(8,128)(2,1)S(1)}, bf16[4,12,16,256]{3,2,1,0:T(8,128)(2,1)S(1)}, u32[]{:S(2)}, u32[]{:S(2)}) collective-permute-start(bf16[4,12,16,256]{3,2,1,0:T(8,128)(2,1)S(1)} %collective-permute-done.11.refs_5_), channel_id=1, source_target_pairs={{0,1},{1,0},{2,3},{3,2},{4,5},{5,4},{6,7},{7,6},{8,9},{9,8},{10,11... | collective-permute-start | bytes 1179656 | tf_op jit(solution)/shard_map/ppermute | solution.py:20
  47.2 16.7 %copy-start.5 = (f32[8]{0:T(128)S(1)}, f32[8]{0:T(128)}, u32[]{:S(2)}) copy-start(f32[8]{0:T(128)} %param.17) | copy-start | bytes 100
  57.4 11.0 %collective-permute-start.15 = (bf16[256,256]{1,0:T(8,128)(2,1)S(1)}, bf16[256,256]{1,0:T(8,128)(2,1)S(1)}, u32[]{:S(2)}, u32[]{:S(2)}) collective-permute-start(bf16[256,256]{1,0:T(8,128)(2,1)S(1)} %get-tuple-element.59), channel_id=1, source_target_pairs={{0,1},{1,2},{2,3},{3,4},{4,5},{5,6},{6,7},{7,8},{8,9},{9,10},{10,1... | collective-permute-start | bytes 393224 | tf_op jit(solution)/shard_map/ppermute | solution.py:20
  59.4 9.0 %collective-permute-start.16 = (bf16[256,256]{1,0:T(8,128)(2,1)S(1)}, bf16[256,256]{1,0:T(8,128)(2,1)S(1)}, u32[]{:S(2)}, u32[]{:S(2)}) collective-permute-start(bf16[256,256]{1,0:T(8,128)(2,1)S(1)} %get-tuple-element.60), channel_id=1, source_target_pairs={{1,0},{2,1},{3,2},{4,3},{5,4},{6,5},{7,6},{8,7},{9,8},{10,9},{11,1... | collective-permute-start | bytes 393224 | tf_op jit(solution)/shard_map/ppermute | solution.py:20
